TPU v7x, 128 devices: a whole 4x4x4 slice. The times are simulated.
128 devices in a mesh: member: 8 (over y, x_hi), space: 8 (over z, x_lo), step: 2 (over core).
Axes of the slice: x: 4 (x_hi: 2, x_lo: 2; x = x_hi * 2 + x_lo), y: 4, z: 4, core: 2. Of those that a mesh axis runs over, the one named last changes fastest.
Arguments:
- state: bfloat16 [16, 2048, 1024], P('member', 'space'), may hold values from -6 to 6
- norm_gain: float32 [1024], replicated, may hold values from 0.5 to 1.5
- w_query: bfloat16 [1024, 1024], replicated, may hold values from -2 to 2
- w_key: bfloat16 [1024, 1024], replicated, may hold values from -2 to 2
- w_value: bfloat16 [1024, 1024], replicated, may hold values from -0.1875 to 0.1875
- w_out: bfloat16 [1024, 1024], replicated, may hold values from -0.1875 to 0.1875
- w_decode: bfloat16 [1024, 128], replicated, may hold values from -0.1875 to 0.1875
- neighbours: int32 [16, 4], P('space'), may hold values from 0 to 15, as said below
- counts: int32 [16], P('space'), may hold values from 2 to 4
- group_ids: int32 [128], replicated, may hold values from 0 to 7, as said below
- area: float32 [2048], P('space'), may hold values from 0.3 to 9
- truth: bfloat16 [2, 2048, 128], P('step', 'space'), may hold values from -6 to 6
Outputs:
- new_state: bfloat16 [2, 16, 2048, 1024], P('step', 'member', 'space')
- losses: float32 [2, 8], P('step')
Inputs may be any that keep to these rules, and one draw needn't show every extreme that they name: neighbours[b, 0] = b; every other entry lies within 2 blocks of b, and entries reach that distance. `group_ids`: each group holds exactly 16 variables.
All inputs are finite; a program needn't handle non-finite values.
Results may differ from a plain program's by a relative error of at most 0.0065.
Values may be sent and summed in bfloat16 or wider, within the bound.
A program may use at most 128 MiB of HBM per device.

v0:
```python
import math

import jax
import jax.numpy as jnp
from jax import lax
from jax.sharding import PartitionSpec as P

HEAD = 64
VARS = 128
GROUPS = 8


alpha_fair = 0.95


def extended(block, sides, width):
    for axis, dim in sides:
        count = lax.axis_size(axis)
        forward = [(i, i + 1) for i in range(count - 1)]
        backward = [(target, source) for source, target in forward]
        low = lax.ppermute(
            lax.slice_in_dim(block, block.shape[dim] - width, None, axis=dim), axis, forward
        )
        high = lax.ppermute(lax.slice_in_dim(block, 0, width, axis=dim), axis, backward)
        block = jnp.concatenate([low, block, high], axis=dim)
    return block


def from_behind(value, axis, steps):
    count = lax.axis_size(axis)
    leading, last = (max(0, -steps), min(count, count - steps))
    return lax.ppermute(value, axis, [(source, source + steps) for source in range(leading, last)])


def rms_normed(fields, gain):
    values = fields.astype(jnp.float32)
    factor = lax.rsqrt(jnp.mean(values * values, axis=-1, keepdims=True) + 1e-06)
    return (values * factor * gain).astype(jnp.bfloat16)


def project(rows, weight):
    return jnp.einsum("mpd,de->mpe", rows, weight, preferred_element_type=jnp.float32).astype(
        jnp.bfloat16
    )


def attend(fields, norm_gain, w_query, w_key, w_value, w_out, neighbours, counts, space_index):
    members, rows, width = fields.shape
    blocks, slots = neighbours.shape
    block_rows = rows // blocks
    heads = width // HEAD
    normed = rms_normed(fields, norm_gain)
    queries = project(normed, w_query)
    local_pair = jnp.stack((project(normed, w_key), project(normed, w_value)), axis=2)
    paired = extended(local_pair, (("space", 1),), rows)
    paired = paired.reshape(members, 3 * blocks, block_rows, 2, width)
    local_index = (neighbours - (space_index * blocks - blocks)).reshape(-1)
    picked = jnp.take(paired, local_index, axis=1)
    picked = picked.reshape(members, blocks, slots * block_rows, 2, heads, HEAD)
    query_blocks = queries.reshape(members, blocks, block_rows, heads, HEAD)
    scores = jnp.einsum(
        "mbqhe,mbkhe->mbhqk", query_blocks, picked[:, :, :, 0], preferred_element_type=jnp.float32
    )
    scores = scores / math.sqrt(HEAD)
    valid = jnp.repeat(jnp.arange(slots)[None, :] < counts[:, None], block_rows, axis=1)
    scores = jnp.where(valid[None, :, None, None, :], scores, -1e30)
    highest = jnp.max(scores, axis=-1, keepdims=True)
    raised = jnp.exp(scores - highest)
    probs = (raised / jnp.sum(raised, axis=-1, keepdims=True)).astype(jnp.bfloat16)
    attended = jnp.einsum(
        "mbhqk,mbkhe->mbqhe", probs, picked[:, :, :, 1], preferred_element_type=jnp.float32
    )
    attended = attended.astype(jnp.bfloat16).reshape(members, rows, width)
    update = jnp.einsum("mpd,de->mpe", attended, w_out, preferred_element_type=jnp.float32)
    return (fields.astype(jnp.float32) + update).astype(jnp.bfloat16)


def crps_terms(preds, target):
    values = preds.astype(jnp.float32)
    goal = target.astype(jnp.float32)
    members = values.shape[0]
    skill = jnp.mean(jnp.abs(values - goal[None]), axis=0)
    spread = jnp.sum(jnp.abs(values[:, None] - values[None, :]), axis=(0, 1))
    epsilon = (1.0 - alpha_fair) / members
    return skill - (1.0 - epsilon) * spread / (2.0 * members * (members - 1))


def group_sums(terms, area_rows, group_ids):
    onehot = (group_ids[:, None] == jnp.arange(GROUPS)[None, :]).astype(jnp.float32)
    weighted = jnp.dot(area_rows, terms, precision=lax.Precision.HIGHEST)
    return (jnp.dot(weighted, onehot, precision=lax.Precision.HIGHEST), jnp.sum(area_rows))


def shards(
    state,
    norm_gain,
    w_query,
    w_key,
    w_value,
    w_out,
    w_decode,
    neighbours,
    counts,
    group_ids,
    area,
    truth,
):
    section_index = lax.axis_index("step")
    section_count = lax.axis_size("step")
    space_index = lax.axis_index("space")
    current = jnp.where(section_index == 0, state, jnp.zeros_like(state))
    final = jnp.zeros_like(state)
    for tick in range(section_count):
        result = attend(
            current, norm_gain, w_query, w_key, w_value, w_out, neighbours, counts, space_index
        )
        final = jnp.where(section_index == tick, result, final)
        if tick + 1 < section_count:
            current = from_behind(result, "step", 1)
    preds = jnp.einsum("mpd,dv->mpv", final, w_decode, preferred_element_type=jnp.float32).astype(
        jnp.bfloat16
    )
    every_member = lax.all_gather(preds, "member", axis=0, tiled=True)
    partial_sums, area_total = group_sums(crps_terms(every_member, truth[0]), area, group_ids)
    totals, area_sum = lax.psum((partial_sums, area_total), "space")
    losses = totals / (area_sum * (VARS // GROUPS))
    return (final[None], losses[None])


def solution(mesh):
    return jax.shard_map(
        shards,
        mesh=mesh,
        in_specs=(
            P("member", "space", None),
            P(),
            P(),
            P(),
            P(),
            P(),
            P(),
            P("space", None),
            P("space"),
            P(),
            P("space"),
            P("step", "space", None),
        ),
        out_specs=(P("step", "member", "space", None), P("step", None)),
        check_vma=False,
    )
```

profile of v0, /device:TPU:1, one launch (start us, length us, event | category | flops | bytes accessed | tf_op | source)
XLA Modules:
  0.0 499.6 jit_solution(5384662600399997927)
XLA Ops:
  8.8 2.0 fusion.73
  10.8 1.3 fusion.67
  13.1 1.5 pad_maximum_fusion.2
  14.6 5.3 %collective-permute-start = (bf16[2,256,2,1024]{3,1,0,2:T(8,128)(2,1)}, bf16[2,256,2,1024]{3,1,0,2:T(8,128)(2,1)}, u32[]{:S(2)}, u32[]{:S(2)}) collective-permute-start(bf16[2,256,2,1024]{3,1,0,2:T(8,128)(2,1)} %pad_maximum_fusion.2), channel_id=1, source_target_pairs={{0,2},{2,4},{4,6},{6,8},{8,10},{10,12},{12,14},{1,3},{3,5},{5,7},{... | collective-permute-start | bytes 6291464 | tf_op jit(solution)/shard_map/ppermute | solution.py:21
  19.9 1.3 collective-permute-start.1
  21.3 3.9 fusion.54
  25.2 4.4 reshape.104
  29.7 32.5 %collective-permute-done = bf16[2,256,2,1024]{3,1,0,2:T(8,128)(2,1)} collective-permute-done((bf16[2,256,2,1024]{3,1,0,2:T(8,128)(2,1)}, bf16[2,256,2,1024]{3,1,0,2:T(8,128)(2,1)}, u32[]{:S(2)}, u32[]{:S(2)}) %collective-permute-start) | collective-permute-done | bytes 2097184 | tf_op jit(solution)/shard_map/ppermute | solution.py:21
  62.2 47.3 %collective-permute-done.1 = bf16[2,256,2,1024]{3,1,0,2:T(8,128)(2,1)} collective-permute-done((bf16[2,256,2,1024]{3,1,0,2:T(8,128)(2,1)}, bf16[2,256,2,1024]{3,1,0,2:T(8,128)(2,1)}, u32[]{:S(2)}, u32[]{:S(2)}) %collective-permute-start.1) | collective-permute-done | bytes 2097184 | tf_op jit(solution)/shard_map/ppermute | solution.py:24
  109.5 3.6 pad_maximum_fusion
  113.1 3.4 copy.60
  116.4 7.4 %gather_fusion = bf16[8,2,128,2,1024]{4,2,3,1,0:T(8,128)(2,1)} fusion(bf16[2,6,128,2,1024]{4,2,3,1,0:T(8,128)(2,1)} %copy.60, s32[1024]{0:T(1024)S(1)} %pad_clamp_fusion), kind=kCustom, calls=%fused_computation.clone | custom fusion | bytes 16777248 | tf_op jit(solution)/shard_map/jit(_take)/gather | solution.py:58
  123.8 7.5 %select_bitcast_fusion.1 = bf16[2,8,128,2,1024]{4,2,3,0,1:T(8,128)(2,1)} fusion(bf16[8,2,128,2,1024]{4,2,3,1,0:T(8,128)(2,1)} %gather_fusion, pred[8]{0:T(512)(128)(4,1)S(1)} %compare_and_fusion), kind=kLoop, calls=%fused_computation.14 | loop fusion | flops 4194304 | bytes 16777224 | tf_op jit(solution)/shard_map/jit(_take)/select_n | solution.py:58
  131.3 12.4 %copy.61 = bf16[2,8,128,2,1024]{2,1,4,3,0:T(8,128)(2,1)} copy(bf16[2,8,128,2,1024]{4,2,3,0,1:T(8,128)(2,1)} %select_bitcast_fusion.1) | data formatting | bytes 16777216 | tf_op jit(solution)/shard_map/jit(_take)/select_n | solution.py:58
  143.7 13.1 %reshape.65 = bf16[2,2,512,2,16,64]{2,1,5,4,3,0:T(2,128)(2,1)} reshape(bf16[2,8,128,2,1024]{2,1,4,3,0:T(8,128)(2,1)} %copy.61) | data formatting | bytes 16777216 | tf_op jit(solution)/shard_map/reshape | solution.py:59
  156.8 8.2 %fusion.104 = (bf16[2,2,512,1,16,64]{2,1,5,4,3,0:T(2,128)(2,1)}, bf16[2,2,512,1,16,64]{2,1,5,4,3,0:T(2,128)(2,1)S(1)}) fusion(bf16[2,2,512,2,16,64]{2,1,5,4,3,0:T(2,128)(2,1)} %reshape.65), kind=kLoop, calls=%fused_computation.114 | loop fusion | bytes 16777216 | tf_op jit(solution)/shard_map/slice | solution.py:71
  164.9 8.0 %fusion.13 = f32[2,2,16,128,512]{4,3,2,1,0:T(8,128)} fusion(bf16[2,2,512,1,16,64]{2,1,5,4,3,0:T(2,128)(2,1)S(1)} %get-tuple-element.8, bf16[2,2,128,16,64]{4,3,2,1,0:T(8,128)(2,1)S(1)} %copy-done.2), kind=kOutput, calls=%fused_computation.29 | convolution fusion | flops 536870912 | bytes 22020096 | tf_op jit(solution)/shard_map/mbqhe,mbkhe->mbhqk/dot_general | solution.py:61
  173.0 19.1 %fusion.105 = (f32[2,2,16,128]{3,2,1,0:T(8,128)S(1)}, f32[2,2,16,128,512]{4,3,2,1,0:T(8,128)}) fusion(f32[2,2,16,128,512]{4,3,2,1,0:T(8,128)} %fusion.13, pred[2,512]{1,0:T(4,128)(4,1)S(1)} %bitcast.125), kind=kOutput, calls=%fused_computation.115 | output fusion | flops 25166336 | bytes 33588224 | tf_op jit(solution)/shard_map/sub | solution.py:68
  192.1 21.1 %fusion.76 = bf16[2,2,128,16,64]{2,4,3,1,0:T(8,128)(2,1)S(1)} fusion(f32[2,2,16,128,512]{4,3,2,1,0:T(8,128)} %get-tuple-element.10, f32[2,2,16,128]{3,2,1,0:T(8,128)S(1)} %get-tuple-element.9, bf16[2,2,512,1,16,64]{2,1,5,4,3,0:T(2,128)(2,1)} %get-tuple-element.7), kind=kOutput, calls=%fused_computation.78 | convolution fusion | flops 545783808 | bytes 22052864 | tf_op jit(solution)/shard_map/mbhqk,mbkhe->mbqhe/dot_general | solution.py:70
  214.3 1.5 reshape.106
  215.8 3.2 fusion.17
  219.0 1.6 collective-permute-start.2
  220.6 4.8 collective-permute-done.2
  225.7 1.3 fusion.70
  227.1 1.3 fusion.64
  228.4 1.5 pad_maximum_fusion.3
  229.9 4.5 collective-permute-start.3
  234.4 1.3 collective-permute-start.4
  235.7 3.9 fusion.57
  239.6 2.9 reshape.107
  242.6 35.7 %collective-permute-done.3 = bf16[2,256,2,1024]{3,1,0,2:T(8,128)(2,1)} collective-permute-done((bf16[2,256,2,1024]{3,1,0,2:T(8,128)(2,1)}, bf16[2,256,2,1024]{3,1,0,2:T(8,128)(2,1)}, u32[]{:S(2)}, u32[]{:S(2)}) %collective-permute-start.3) | collective-permute-done | bytes 2097184 | tf_op jit(solution)/shard_map/ppermute | solution.py:21
  278.3 47.3 %collective-permute-done.4 = bf16[2,256,2,1024]{3,1,0,2:T(8,128)(2,1)} collective-permute-done((bf16[2,256,2,1024]{3,1,0,2:T(8,128)(2,1)}, bf16[2,256,2,1024]{3,1,0,2:T(8,128)(2,1)}, u32[]{:S(2)}, u32[]{:S(2)}) %collective-permute-start.4) | collective-permute-done | bytes 2097184 | tf_op jit(solution)/shard_map/ppermute | solution.py:24
  325.6 3.6 pad_maximum_fusion.1
  329.1 3.4 copy.68
  332.5 7.4 %gather_fusion.1 = bf16[8,2,128,2,1024]{4,2,3,1,0:T(8,128)(2,1)} fusion(bf16[2,6,128,2,1024]{4,2,3,1,0:T(8,128)(2,1)} %copy.68, s32[1024]{0:T(1024)S(1)} %pad_clamp_fusion), kind=kCustom, calls=%fused_computation.1.clone | custom fusion | bytes 16777248 | tf_op jit(solution)/shard_map/jit(_take)/gather | solution.py:58
  339.9 7.5 %select_bitcast_fusion = bf16[2,8,128,2,1024]{4,2,3,0,1:T(8,128)(2,1)} fusion(bf16[8,2,128,2,1024]{4,2,3,1,0:T(8,128)(2,1)} %gather_fusion.1, pred[8]{0:T(512)(128)(4,1)S(1)} %compare_and_fusion), kind=kLoop, calls=%fused_computation.13 | loop fusion | flops 4194304 | bytes 16777224 | tf_op jit(solution)/shard_map/jit(_take)/select_n | solution.py:58
  347.3 12.4 %copy.69 = bf16[2,8,128,2,1024]{2,1,4,3,0:T(8,128)(2,1)} copy(bf16[2,8,128,2,1024]{4,2,3,0,1:T(8,128)(2,1)} %select_bitcast_fusion) | data formatting | bytes 16777216 | tf_op jit(solution)/shard_map/jit(_take)/select_n | solution.py:58
  359.7 13.1 %reshape.69 = bf16[2,2,512,2,16,64]{2,1,5,4,3,0:T(2,128)(2,1)} reshape(bf16[2,8,128,2,1024]{2,1,4,3,0:T(8,128)(2,1)} %copy.69) | data formatting | bytes 16777216 | tf_op jit(solution)/shard_map/reshape | solution.py:59
  372.8 8.0 %fusion.103 = (bf16[2,2,512,1,16,64]{2,1,5,4,3,0:T(2,128)(2,1)}, bf16[2,2,512,1,16,64]{2,1,5,4,3,0:T(2,128)(2,1)S(1)}) fusion(bf16[2,2,512,2,16,64]{2,1,5,4,3,0:T(2,128)(2,1)} %reshape.69), kind=kLoop, calls=%fused_computation.113 | loop fusion | bytes 16777216 | tf_op jit(solution)/shard_map/slice | solution.py:71
  380.8 8.0 %fusion.12 = f32[2,2,16,128,512]{4,3,2,1,0:T(8,128)} fusion(bf16[2,2,512,1,16,64]{2,1,5,4,3,0:T(2,128)(2,1)S(1)} %get-tuple-element.6, bf16[2,2,128,16,64]{4,3,2,1,0:T(8,128)(2,1)S(1)} %reshape.107), kind=kOutput, calls=%fused_computation.26 | convolution fusion | flops 536870912 | bytes 22020096 | tf_op jit(solution)/shard_map/mbqhe,mbkhe->mbhqk/dot_general | solution.py:61
  388.9 19.1 %fusion.106 = (f32[2,2,16,128]{3,2,1,0:T(8,128)S(1)}, f32[2,2,16,128,512]{4,3,2,1,0:T(8,128)}) fusion(f32[2,2,16,128,512]{4,3,2,1,0:T(8,128)} %fusion.12, pred[2,512]{1,0:T(4,128)(4,1)S(1)} %bitcast.126), kind=kOutput, calls=%fused_computation.116 | output fusion | flops 25166336 | bytes 33588224 | tf_op jit(solution)/shard_map/sub | solution.py:68
  408.0 9.0 %fusion.77 = bf16[2,2,128,16,64]{2,4,3,1,0:T(8,128)(2,1)S(1)} fusion(f32[2,2,16,128,512]{4,3,2,1,0:T(8,128)} %get-tuple-element.12, f32[2,2,16,128]{3,2,1,0:T(8,128)S(1)} %get-tuple-element.11, bf16[2,2,512,1,16,64]{2,1,5,4,3,0:T(2,128)(2,1)} %get-tuple-element.5), kind=kOutput, calls=%fused_computation.79 | convolution fusion | flops 545783808 | bytes 22052864 | tf_op jit(solution)/shard_map/mbhqk,mbkhe->mbqhe/dot_general | solution.py:70
  418.1 1.5 reshape.109
  419.6 3.3 fusion.78
  424.7 44.8 %all-gather.2.cloned.1.call-done = bf16[16,256,128]{2,1,0:T(8,128)(2,1)} async-done(((bf16[2,256,128]{2,1,0:T(8,128)(2,1)}), bf16[16,256,128]{2,1,0:T(8,128)(2,1)}) %all-gather.2.cloned.1.call-update) | async-done | bytes 1048592 | tf_op jit(solution)/shard_map/all_gather | solution.py:123
  469.5 1.5 convert_element_type.84
  471.1 3.4 abs_reduce_fusion
  475.1 16.2 %all-reduce = (f32[8]{0:T(128)S(1)}, f32[]{:T(128)}) all-reduce(f32[8]{0:T(128)S(1)} %convolution_bitcast_fusion, f32[]{:T(128)} %reduce_sum.69), channel_id=1, replica_groups=mesh['member'=8,'space'=8,'step'=2] {'space'}, use_global_device_ids=true, to_apply=%region_8.10 | all-reduce | flops 9 | bytes 72 | tf_op jit(solution)/shard_map/psum | solution.py:125
  (65 shorter events, 8.2 us)
Async XLA Ops:
  7.2 1.6 copy-start
  7.2 3.6 copy-start.18
  7.2 462.4 %all-gather.2.cloned.1.call-start = ((), (), s32[]{:S(2)}) async-start(), calls=%async_computation | async-start | bytes 1179648 | tf_op jit(solution)/shard_map/all_gather | solution.py:123
  7.2 3.5 copy-start.6
  7.3 3.5 copy-start.15
  10.8 10.4 %copy-start.14 = (s32[2,4]{1,0:T(2,128)S(1)}, s32[2,4]{1,0:T(2,128)}, u32[]{:S(2)}) copy-start(s32[2,4]{1,0:T(2,128)} %param.21) | copy-start | bytes 100
  12.1 1.0 copy-start.4
  14.6 47.6 %collective-permute-start = (bf16[2,256,2,1024]{3,1,0,2:T(8,128)(2,1)}, bf16[2,256,2,1024]{3,1,0,2:T(8,128)(2,1)}, u32[]{:S(2)}, u32[]{:S(2)}) collective-permute-start(bf16[2,256,2,1024]{3,1,0,2:T(8,128)(2,1)} %pad_maximum_fusion.2), channel_id=1, source_target_pairs={{0,2},{2,4},{4,6},{6,8},{8,10},{10,12},{12,14},{1,3},{3,5},{5,7},{... | collective-permute-start | bytes 6291464 | tf_op jit(solution)/shard_map/ppermute | solution.py:21
  19.9 89.6 %collective-permute-start.1 = (bf16[2,256,2,1024]{3,1,0,2:T(8,128)(2,1)}, bf16[2,256,2,1024]{3,1,0,2:T(8,128)(2,1)}, u32[]{:S(2)}, u32[]{:S(2)}) collective-permute-start(bf16[2,256,2,1024]{3,1,0,2:T(8,128)(2,1)} %pad_maximum_fusion.2), channel_id=1, source_target_pairs={{2,0},{4,2},{6,4},{8,6},{10,8},{12,10},{14,12},{3,1},{5,3},{7,5},{... | collective-permute-start | bytes 6291464 | tf_op jit(solution)/shard_map/ppermute | solution.py:24
  21.3 8.3 %copy-start.19 = (s32[2]{0:T(128)S(1)}, s32[2]{0:T(128)}, u32[]{:S(2)}) copy-start(s32[2]{0:T(128)} %param.22) | copy-start | bytes 28
  156.8 8.2 %copy-start.2 = (bf16[2,2,128,16,64]{4,3,2,1,0:T(8,128)(2,1)S(1)}, bf16[2,2,128,16,64]{4,3,2,1,0:T(8,128)(2,1)}, u32[]{:S(2)}) copy-start(bf16[2,2,128,16,64]{4,3,2,1,0:T(8,128)(2,1)} %reshape.104) | copy-start | bytes 3145732
  219.0 8.1 %copy-start.17 = (bf16[2,256,1024]{2,1,0:T(8,128)(2,1)}, bf16[2,256,1024]{2,1,0:T(8,128)(2,1)S(1)}, u32[]{:S(2)}) copy-start(bf16[2,256,1024]{2,1,0:T(8,128)(2,1)S(1)} %fusion.17) | copy-start | bytes 3145732
  219.0 8.1 %copy-start.16 = (bf16[1024,1024]{1,0:T(8,128)(2,1)S(1)}, bf16[1024,1024]{1,0:T(8,128)(2,1)}, u32[]{:S(2)}) copy-start(bf16[1024,1024]{1,0:T(8,128)(2,1)} %param.18) | copy-start | bytes 6291460
  219.0 6.4 %collective-permute-start.2 = (bf16[2,256,1024]{2,1,0:T(8,128)(2,1)S(1)}, bf16[2,256,1024]{2,1,0:T(8,128)(2,1)S(1)}, u32[]{:S(2)}, u32[]{:S(2)}) collective-permute-start(bf16[2,256,1024]{2,1,0:T(8,128)(2,1)S(1)} %fusion.17), channel_id=1, source_target_pairs={{0,1},{2,3},{4,5},{6,7},{8,9},{10,11},{12,13},{14,15},{16,17},{18,... | collective-permute-start | bytes 3145736 | tf_op jit(solution)/shard_map/ppermute | solution.py:32
  225.4 1.6 copy-start.7
  228.4 7.3 %copy-start.5 = (bf16[2,256,1,1024]{3,1,0,2:T(8,128)(2,1)}, bf16[2,256,1,1024]{3,1,0,2:T(8,128)(2,1)S(1)}, u32[]{:S(2)}) copy-start(bf16[2,256,1,1024]{3,1,0,2:T(8,128)(2,1)S(1)} %fusion.64) | copy-start | bytes 3145732
  228.4 7.3 %copy-start.8 = (bf16[2,256,1024]{2,1,0:T(8,128)(2,1)S(1)}, bf16[2,256,1024]{2,1,0:T(8,128)(2,1)}, u32[]{:S(2)}) copy-start(bf16[2,256,1024]{2,1,0:T(8,128)(2,1)} %copy-done.7) | copy-start | bytes 3145732
  229.9 48.4 %collective-permute-start.3 = (bf16[2,256,2,1024]{3,1,0,2:T(8,128)(2,1)}, bf16[2,256,2,1024]{3,1,0,2:T(8,128)(2,1)}, u32[]{:S(2)}, u32[]{:S(2)}) collective-permute-start(bf16[2,256,2,1024]{3,1,0,2:T(8,128)(2,1)} %pad_maximum_fusion.3), channel_id=1, source_target_pairs={{0,2},{2,4},{4,6},{6,8},{8,10},{10,12},{12,14},{1,3},{3,5},{5,7},{... | collective-permute-start | bytes 6291464 | tf_op jit(solution)/shard_map/ppermute | solution.py:21
  234.4 91.2 %collective-permute-start.4 = (bf16[2,256,2,1024]{3,1,0,2:T(8,128)(2,1)}, bf16[2,256,2,1024]{3,1,0,2:T(8,128)(2,1)}, u32[]{:S(2)}, u32[]{:S(2)}) collective-permute-start(bf16[2,256,2,1024]{3,1,0,2:T(8,128)(2,1)} %pad_maximum_fusion.3), channel_id=1, source_target_pairs={{2,0},{4,2},{6,4},{8,6},{10,8},{12,10},{14,12},{3,1},{5,3},{7,5},{... | collective-permute-start | bytes 6291464 | tf_op jit(solution)/shard_map/ppermute | solution.py:24
  417.0 2.6 copy-start.9
  419.6 3.3 copy-start.11
  419.6 4.5 copy-start.13
  419.6 5.1 %copy-start.12 = (bf16[1,256,128]{2,1,0:T(8,128)(2,1)S(1)}, bf16[1,256,128]{2,1,0:T(8,128)(2,1)}, u32[]{:S(2)}) copy-start(bf16[1,256,128]{2,1,0:T(8,128)(2,1)} %param.25) | copy-start | bytes 196612
  422.9 51.5 %copy-start.10 = (bf16[2,256,1024]{2,1,0:T(8,128)(2,1)}, bf16[2,256,1024]{2,1,0:T(8,128)(2,1)S(1)}, u32[]{:S(2)}) copy-start(bf16[2,256,1024]{2,1,0:T(8,128)(2,1)S(1)} %fusion.78) | copy-start | bytes 3145732
  424.7 67.9 %copy-start.1 = (bf16[1024,1024]{1,0:T(8,128)(2,1)S(1)}, bf16[1024,1024]{1,0:T(8,128)(2,1)}, u32[]{:S(2)}) copy-start(bf16[1024,1024]{1,0:T(8,128)(2,1)} %param.17) | copy-start | bytes 6291460
  424.7 50.3 %copy-start.20 = (s32[128]{0:T(128)S(1)}, s32[128]{0:T(128)}, u32[]{:S(2)}) copy-start(s32[128]{0:T(128)} %param.23) | copy-start | bytes 1540
  469.5 4.9 copy-start.3
Sparse Core Ops, SparseCore 0:
  424.2 45.3 all-gather.1
where the time goes:
time: 509 us; the launch traced here: 500 us
  waiting for transfers between devices  212 us (42%)
  local copies, waits for them, and re-layouts  103 us (20%)
  other arithmetic  70.3 us (14%)
  matrix products  67.9 us (13%)
  blocking collectives  16.2 us (3%)
  between operations  15.3 us (3%)
  starting transfers between devices  13.9 us (3%)
    ppermute x2, waiting for transfers between devices, extended(): lax.ppermute(lax.slice_in_dim(block, 0, width, axis=dim), axis, backward)  94.6 us
    ppermute x2, waiting for transfers between devices, extended(): lax.ppermute(lax.slice_in_dim(block, block.shape[dim] - width, None, axis...  68.2 us
    all_gather x1, waiting for transfers between devices, shards(): every_member = lax.all_gather(preds, 'member', axis=0, tiled=True)  44.8 us
    sub x2, other arithmetic, attend(): raised = jnp.exp(scores - highest)  38.2 us
    dot_general x2, matrix products, attend(): jnp.einsum('mbhqk,mbkhe->mbqhe', probs, picked[:, :, :, 1], preferred_ele...  30.1 us
    reshape x2, local copies, waits for them, and re-layouts, attend(): picked = picked.reshape(members, blocks, slots * block_rows, 2, heads, HEAD)  26.2 us
    select_n x2, local copies, waits for them, and re-layouts, attend(): picked = jnp.take(paired, local_index, axis=1)  24.8 us
    psum x1, blocking collectives, shards(): totals, area_sum = lax.psum((partial_sums, area_total), 'space')  16.2 us
  transfers between devices with their start and end apart: 6, of which 6 were waited for; matrix products, arithmetic and copies ran while one was open for 3% of the time, Pallas kernels for 0%

commit v1 on v0

v1 whole, which is shorter than its diff:
```python
import functools

import jax
import jax.numpy as jnp
from jax import lax
from jax.experimental import pallas as pl
from jax.experimental.pallas import tpu as pltpu
from jax.sharding import PartitionSpec as P

D = 1024
HEAD = 64
VARS = 128
GROUPS = 8
BLOCK = 128
ROWS = 256
MEMBERS = 16
SLOTS = 4
STEPS = 2
ALPHA = 0.95
CHUNKS = 4
CHUNK = ROWS // CHUNKS
TILE = 256
SHARE = 32
MESH = pl.DeviceIdType.MESH
BF = jnp.bfloat16
F32 = jnp.float32


def dot(a, b):
    return jnp.dot(a, b, preferred_element_type=F32)


def dot_t(a, b):
    return lax.dot_general(a, b, (((1,), (1,)), ((), ())), preferred_element_type=F32)


def kernel(
    state, gain, w_query, w_key, w_value, w_out, w_decode, neighbours, counts, group_ids, area, truth,
    out, loss,
    cur, halo, nrm, wbuf, wdec, qkv0, qkv1, att, preds, gathered, goal, gains, groups, areas, meta_v, used_v, meta_s,
    red1, red2,
    lsem, xs, xr, zs, zr, ks, kr, osend, orecv, ps, pr, ms, mr, r1s, r1r, r2s, r2r,
):
    m, s, c = (lax.axis_index(name) for name in ("member", "space", "step"))
    z, xl = lax.div(s, 2), lax.rem(s, 2)
    local = xl == c
    foreign = xl != c
    partner = {"space": 2 * z + 1 - xl}
    other = {"step": 1 - c}
    has_z = jnp.where(c == 1, z < 3, z > 0)
    z_target = {"space": s + 4 * c - 2, "step": 1 - c}
    qkvs = (qkv0, qkv1)

    def fetch(i, src, dst):
        return pltpu.make_async_copy(src, dst, lsem.at[i])

    loads = [
        fetch(0, w_key, wbuf.at[1]),
        fetch(1, w_value, wbuf.at[2]),
        fetch(2, w_query, wbuf.at[0]),
        fetch(3, w_out, wbuf.at[3]),
        fetch(4, w_decode, wdec),
        fetch(5, gain, gains),
        fetch(6, group_ids, groups),
        fetch(7, area, areas),
        fetch(8, truth.at[0, pl.ds(pl.multiple_of(m * SHARE, SHARE), SHARE)], goal),
    ]

    def own_chunk(i):
        part = pl.ds(i * CHUNK, CHUNK)
        return pltpu.make_async_copy(state.at[xl, part], cur.at[0, part], xr.at[i])

    def x_chunk(i):
        part = pl.ds(i * CHUNK, CHUNK)
        return pltpu.make_async_remote_copy(
            state.at[1 - xl, part], cur.at[0, part], xs.at[i], xr.at[i], device_id=partner, device_id_type=MESH
        )

    def z_part(t, i, size):
        part = pl.ds(i * size, size)
        return pltpu.make_async_remote_copy(
            cur.at[t, part], halo.at[t, part], zs.at[t, i], zr.at[t, i], device_id=z_target, device_id_type=MESH
        )

    def meta_copy():
        return pltpu.make_async_remote_copy(
            meta_v.at[0], meta_v.at[1], ms.at[0], mr.at[0], device_id=partner, device_id_type=MESH
        )

    def kv_copy(t, j):
        return pltpu.make_async_remote_copy(
            qkvs[t].at[j, pl.ds(2, 2)],
            qkvs[t].at[j, pl.ds(4 * c, 2)],
            ks.at[t, j - 1], kr.at[t, j - 1], device_id=other, device_id_type=MESH,
        )

    def out_remote(t, b, slot):
        part = pl.ds(b * BLOCK, BLOCK)
        return pltpu.make_async_remote_copy(
            cur.at[t + 1, part], out.at[0, slot, part], osend.at[t, b], orecv.at[slot, b],
            device_id={"space": 2 * z + c, "step": t}, device_id_type=MESH,
        )

    def out_local(t, b, slot):
        part = pl.ds(b * BLOCK, BLOCK)
        return pltpu.make_async_copy(cur.at[t + 1, part], out.at[0, slot, part], orecv.at[slot, b])

    def preds_copy(t, i):
        return pltpu.make_async_remote_copy(
            preds.at[t, pl.ds(i * SHARE, SHARE)], gathered.at[2 * m + xl], ps.at[t, i], pr.at[0],
            device_id={"member": i, "space": 2 * z + c, "step": t}, device_id_type=MESH,
        )

    def preds_own(t, i):
        return pltpu.make_async_copy(preds.at[t, pl.ds(i * SHARE, SHARE)], gathered.at[2 * m + xl], pr.at[0])

    barrier = pltpu.get_barrier_semaphore()

    def greet(**device):
        pl.semaphore_signal(barrier, inc=1, device_id=device, device_id_type=MESH)

    for copy in loads[:1]:
        copy.start()

    def greet_plane(i, _):
        mate = lax.rem(m + lax.div(i, 4), 8)
        x_mate = lax.rem(xl + lax.rem(lax.div(i, 2), 2), 2)
        core = lax.rem(c + lax.rem(i, 2), 2)
        greet(member=mate, space=2 * z + x_mate, step=core)
        return 0

    lax.fori_loop(1, 32, greet_plane, 0)
    for dz in range(1, 4):
        for x_mate in range(2):
            greet(space=2 * lax.rem(z + dz, 4) + x_mate)

    @pl.when(has_z)
    def _():
        greet(**z_target)

    @pl.when(local)
    def _():
        for i in range(CHUNKS):
            own_chunk(i).start()

    for copy in loads[1:]:
        copy.start()

    column = lax.broadcasted_iota(jnp.int32, (8, 128), 1)
    row8 = lax.broadcasted_iota(jnp.int32, (8, 128), 0)
    meta = jnp.zeros((8, 128), jnp.int32)
    for b in range(2):
        for slot in range(SLOTS):
            meta = jnp.where(column == b * SLOTS + slot, neighbours[b, slot], meta)
    meta = jnp.where(row8 == 2, counts[0], jnp.where(row8 == 3, counts[1], meta))
    meta_v[0] = meta

    @pl.when(jnp.logical_not(has_z))
    def _():
        halo[...] = jnp.zeros_like(halo)

    pl.semaphore_wait(barrier, 37 + has_z.astype(jnp.int32))

    @pl.when(local)
    def _():
        for i in range(CHUNKS):
            x_chunk(i).start()
        meta_copy().start()
        to_scalars = pltpu.make_async_copy(meta_v.at[0], meta_s, lsem.at[9])
        to_scalars.start()
        to_scalars.wait()
        used_v[...] = meta_v[0, 2:4, :]

    for i in range(CHUNKS):
        own_chunk(i).wait()

        @pl.when(has_z)
        def _():
            z_part(0, i, CHUNK).start()

    @pl.when(foreign)
    def _():
        meta_copy().wait_recv()
        to_scalars = pltpu.make_async_copy(meta_v.at[1], meta_s, lsem.at[9])
        to_scalars.start()
        to_scalars.wait()
        used_v[...] = meta_v[1, 2:4, :]

    loads[5].wait()

    def normalise(src, row, rows, dst):
        def step(i, _):
            part = pl.ds(pl.multiple_of(row + i * 32, 32), 32)
            values = src[part, :].astype(F32)
            factor = lax.rsqrt(jnp.mean(values * values, axis=-1, keepdims=True) + 1e-06)
            dst[part, :] = (values * factor * gains[...]).astype(BF)
            return 0

        lax.fori_loop(0, rows // 32, step, 0)

    def project(row, rows, w, dst, dst_block):
        def step(n, _):
            cols = pl.ds(pl.multiple_of(n * TILE, TILE), TILE)
            values = dot(nrm[pl.ds(row, rows), :], wbuf[w, :, cols]).astype(BF)
            for i in range(rows // BLOCK):
                dst[w, dst_block + i, :, cols] = values[i * BLOCK : (i + 1) * BLOCK]
            return 0

        lax.fori_loop(0, D // TILE, step, 0)

    first_block = 4 * z + 2 * c - 2
    head_of = lax.broadcasted_iota(jnp.int32, (1, TILE), 1)
    masks = [
        jnp.where((head_of >= HEAD * i) & (head_of < HEAD * (i + 1)), 0.125, 0.0).astype(BF) for i in range(4)
    ]
    lane = lax.broadcasted_iota(jnp.int32, (BLOCK, TILE), 1)

    def attend(qkv, b):
        near = [jnp.clip(meta_s[0, b * SLOTS + slot] - first_block, 0, 5) for slot in range(SLOTS)]
        used = used_v[b : b + 1, :]
        bias = [jnp.where(used > slot, 0.0, -1e30) for slot in range(SLOTS)]

        def step(g, _):
            cols = pl.ds(pl.multiple_of(g * TILE, TILE), TILE)
            query = qkv[0, 2 + b, :, cols]
            query = jnp.concatenate([query * mask for mask in masks], axis=0)
            keys = [jnp.concatenate([qkv[1, near[i + k], :, cols] for k in range(2)], axis=0) for i in (0, 2)]
            values = jnp.concatenate([qkv[2, near[i], :, cols] for i in range(SLOTS)], axis=0)
            first = dot_t(query, keys[0])
            second = dot_t(query, keys[1])
            second = jnp.concatenate([second[:, :BLOCK] + bias[2], second[:, BLOCK:] + bias[3]], axis=1)
            scores = jnp.concatenate([first, second], axis=1)
            highest = jnp.max(scores, axis=-1, keepdims=True)
            raised = jnp.exp(scores - highest)
            total = jnp.sum(raised, axis=-1, keepdims=True)
            mixed = dot(raised.astype(BF), values) * (1.0 / total)
            parts = [mixed[i * BLOCK : (i + 1) * BLOCK] for i in range(4)]
            attended = parts[3]
            for i in (2, 1, 0):
                attended = jnp.where(lane < HEAD * (i + 1), parts[i], attended)
            att[:, cols] = attended.astype(BF)
            return 0

        lax.fori_loop(0, D // TILE, step, 0)

    def update(t, b):
        part = pl.ds(b * BLOCK, BLOCK)

        def step(n, _):
            cols = pl.ds(pl.multiple_of(n * TILE, TILE), TILE)
            values = cur[t, part, cols].astype(F32) + dot(att[...], wbuf[3, :, cols])
            cur[t + 1, part, cols] = values.astype(BF)
            return 0

        lax.fori_loop(0, D // TILE, step, 0)

    for t in range(STEPS):
        qkv = qkvs[t]
        out_here = local & (c == t)
        normalise(cur.at[t], 0, ROWS, nrm)
        for j in (1, 2, 0):
            if t == 0:
                loads[(2, 0, 1)[j]].wait()
            project(0, ROWS, j, qkv, 2)
            if j:
                kv_copy(t, j).start()
        size = CHUNK if t == 0 else BLOCK
        for b in range(2):

            @pl.when(has_z)
            def _():
                for i in range(BLOCK // size):
                    z_part(t, b * (BLOCK // size) + i, size).wait_recv()

            normalise(halo.at[t], b * BLOCK, BLOCK, nrm)
            for j in (1, 2):
                project(b * BLOCK, BLOCK, j, qkv, 4 * c + b)
        for j in (1, 2):
            kv_copy(t, j).wait_recv()
        if t == 0:
            loads[3].wait()
        for b in range(2):
            attend(qkv, b)
            update(t, b)
            if t + 1 < STEPS:

                @pl.when(has_z)
                def _():
                    z_part(t + 1, b, BLOCK).start()

            @pl.when(out_here)
            def _():
                out_local(t, b, xl).start()

            @pl.when(jnp.logical_not(out_here))
            def _():
                out_remote(t, b, xl).start()

        if t == 0:
            loads[4].wait()
        preds[t] = dot(cur[t + 1], wdec[...]).astype(BF)
        for i in range(8):
            own = out_here & (m == i)

            @pl.when(own)
            def _():
                preds_own(t, i).start()

            @pl.when(jnp.logical_not(own))
            def _():
                preds_copy(t, i).start()

    for copy in loads[6:9]:
        copy.wait()
    pltpu.make_async_copy(gathered, gathered, pr.at[0]).wait()
    epsilon = (1.0 - ALPHA) / MEMBERS
    weighted = jnp.zeros((1, VARS), F32)
    mine = lax.broadcasted_iota(jnp.int32, (SHARE, ROWS), 0) + m * SHARE
    spread_out = jnp.where(lax.broadcasted_iota(jnp.int32, (SHARE, ROWS), 1) == mine, areas[...], 0.0)
    weights = jnp.sum(spread_out, axis=1, keepdims=True)
    for i in range(SHARE // 16):
        part = slice(i * 16, i * 16 + 16)
        values = [gathered[k, part, :].astype(F32) for k in range(MEMBERS)]
        wanted = goal[part, :].astype(F32)
        skill = jnp.zeros((16, VARS), F32)
        spread = jnp.zeros((16, VARS), F32)
        for k in range(MEMBERS):
            skill += jnp.abs(values[k] - wanted)
            for j in range(k):
                spread += jnp.abs(values[k] - values[j])
        terms = skill * (1.0 / MEMBERS) - spread * ((1.0 - epsilon) / (MEMBERS * (MEMBERS - 1)))
        weighted += jnp.sum(terms * weights[part], axis=0, keepdims=True)
    row = lax.broadcasted_iota(jnp.int32, (8, VARS), 0)
    tile = jnp.where(row == 0, weighted, jnp.where(row == 1, jnp.sum(weights, axis=0, keepdims=True), 0.0))

    def exchange(tile, buffer, send, recv, me, axis):
        buffer[me] = tile

        def copy(i):
            return pltpu.make_async_remote_copy(
                buffer.at[me], buffer.at[me], send.at[i - 1], recv.at[0],
                device_id={axis: lax.rem(me + i, 8)}, device_id_type=MESH,
            )

        for i in range(1, 8):
            copy(i).start()
        rest = buffer.at[pl.ds(0, 7)]
        pltpu.make_async_copy(rest, rest, recv.at[0]).wait()
        total = buffer[0]
        for i in range(1, 8):
            total += buffer[i]
        return total, copy

    tile, copy1 = exchange(tile, red1, r1s, r1r, m, "member")
    tile, copy2 = exchange(tile, red2, r2s, r2r, s, "space")
    slot = lax.broadcasted_iota(jnp.int32, (1, GROUPS), 1)
    result = jnp.zeros((1, GROUPS), F32)
    for g in range(GROUPS):
        share = jnp.sum(jnp.where(groups[...] == g, tile[0:1], 0.0), axis=1, keepdims=True)
        result = jnp.where(slot == g, share, result)
    loss[...] = result / (tile[1:2, :GROUPS] * (VARS // GROUPS))

    for slot_xl in range(2):
        for b in range(2):
            out_local(0, b, slot_xl).wait()

    @pl.when(local)
    def _():
        for i in range(CHUNKS):
            x_chunk(i).wait_send()
        meta_copy().wait_send()

    @pl.when(has_z)
    def _():
        for i in range(CHUNKS):
            z_part(0, i, CHUNK).wait_send()
        for i in range(2):
            z_part(1, i, BLOCK).wait_send()

    for t in range(STEPS):
        out_here = local & (c == t)
        for j in (1, 2):
            kv_copy(t, j).wait_send()

        @pl.when(jnp.logical_not(out_here))
        def _():
            for b in range(2):
                out_remote(t, b, xl).wait_send()

        for i in range(8):

            @pl.when(jnp.logical_not(out_here & (m == i)))
            def _():
                preds_copy(t, i).wait_send()

    for i in range(1, 8):
        copy1(i).wait_send()
        copy2(i).wait_send()


def shards(
    state, norm_gain, w_query, w_key, w_value, w_out, w_decode, neighbours, counts, group_ids, area, truth
):
    anywhere = pl.BlockSpec(memory_space=pl.ANY)
    scalars = pl.BlockSpec(memory_space=pltpu.SMEM)
    dma = pltpu.SemaphoreType.DMA
    return pl.pallas_call(
        kernel,
        out_shape=(
            jax.ShapeDtypeStruct((1, 2, ROWS, D), BF),
            jax.ShapeDtypeStruct((1, GROUPS), F32),
        ),
        in_specs=[anywhere] * 7 + [scalars] * 2 + [anywhere] * 3,
        out_specs=(anywhere, pl.BlockSpec(memory_space=pltpu.VMEM)),
        scratch_shapes=[
            pltpu.VMEM((STEPS + 1, ROWS, D), BF),
            pltpu.VMEM((STEPS, ROWS, D), BF),
            pltpu.VMEM((ROWS, D), BF),
            pltpu.VMEM((4, D, D), BF),
            pltpu.VMEM((D, VARS), BF),
            pltpu.VMEM((3, 6, BLOCK, D), BF),
            pltpu.VMEM((3, 6, BLOCK, D), BF),
            pltpu.VMEM((BLOCK, D), BF),
            pltpu.VMEM((STEPS, ROWS, VARS), BF),
            pltpu.VMEM((MEMBERS, SHARE, VARS), BF),
            pltpu.VMEM((SHARE, VARS), BF),
            pltpu.VMEM((1, D), F32),
            pltpu.VMEM((1, VARS), jnp.int32),
            pltpu.VMEM((1, ROWS), F32),
            pltpu.VMEM((2, 8, 128), jnp.int32),
            pltpu.VMEM((2, 128), jnp.int32),
            pltpu.SMEM((8, 128), jnp.int32),
            pltpu.VMEM((8, 8, VARS), F32),
            pltpu.VMEM((8, 8, VARS), F32),
            dma((10,)),
            dma((CHUNKS,)),
            dma((CHUNKS,)),
            dma((STEPS, CHUNKS)),
            dma((STEPS, CHUNKS)),
            dma((STEPS, 2)),
            dma((STEPS, 2)),
            dma((STEPS, 2)),
            dma((2, 2)),
            dma((STEPS, 8)),
            dma((1,)),
            dma((1,)),
            dma((1,)),
            dma((7,)),
            dma((1,)),
            dma((7,)),
            dma((1,)),
        ],
        compiler_params=pltpu.CompilerParams(
            collective_id=0, has_side_effects=True, vmem_limit_bytes=60 * 1024 * 1024
        ),
        name="rollout",
    )(
        state, norm_gain.reshape(1, D), w_query, w_key, w_value, w_out, w_decode, neighbours, counts,
        group_ids.reshape(1, VARS), area.reshape(1, ROWS), truth,
    )


def solution(mesh):
    return jax.shard_map(
        shards,
        mesh=mesh,
        in_specs=(
            P("member", "space", None),
            P(),
            P(),
            P(),
            P(),
            P(),
            P(),
            P("space", None),
            P("space"),
            P(),
            P("space"),
            P("step", "space", None),
        ),
        out_specs=(P("step", "member", "space", None), P("step", None)),
        check_vma=False,
    )
```

time: 509 us -> 73.8 us (0.14); the launches traced: 500 us -> 73.6 us
  waiting for transfers between devices: 212 us -> 0 us
  local copies, waits for them, and re-layouts: 103 us -> 2.78 us
  other arithmetic: 70.3 us -> 0 us
  Pallas kernels: 0 us -> 70.2 us
  matrix products: 67.9 us -> 0 us
  blocking collectives: 16.2 us -> 0 us
  between operations: 15.3 us -> 0.65 us
  starting transfers between devices: 13.9 us -> 0 us
    ppermute x5 -> x0, waiting for transfers between devices: 168 us -> none  [the longest x2 94.6 us: extended(): lax.ppermute(lax.slice_in_dim(block, 0, width, axis=dim), axis, backward)]
    pallas_call x0 -> x1, Pallas kernels: none -> 70.2 us  [shards(): pl.pallas_call(kernel, out_shape=(jax.ShapeDtypeStruct((1, 2, ROWS, D), B...]
    dot_general x15 -> x0, matrix products: 67.9 us -> none  [the longest x2 30.1 us: attend(): jnp.einsum('mbhqk,mbkhe->mbqhe', probs, picked[:, :, :, 1], preferred_ele...]
    all_gather x1 -> x0, waiting for transfers between devices: 44.8 us -> none  [shards(): every_member = lax.all_gather(preds, 'member', axis=0, tiled=True)]
    reshape x9 -> x0, local copies, waits for them, and re-layouts: 43.3 us -> none  [the longest x2 26.2 us: attend(): picked = picked.reshape(members, blocks, slots * block_rows, 2, heads, HEAD)]
    sub x4 -> x0, other arithmetic: 38.2 us -> none  [the longest x2 38.2 us: attend(): raised = jnp.exp(scores - highest)]
    select_n x2 -> x0, local copies, waits for them, and re-layouts: 24.8 us -> none  [attend(): picked = jnp.take(paired, local_index, axis=1)]
    psum x1 -> x0, blocking collectives: 16.2 us -> none  [shards(): totals, area_sum = lax.psum((partial_sums, area_total), 'space')]
  transfers between devices with their start and end apart: 6 -> 0, of which waited for: 6 -> 0; matrix products, arithmetic and copies ran while one was open for 3% -> 0% of each run, Pallas kernels for 0% -> 0%
where the time goes in v1:
time: 73.8 us; the launch traced here: 73.6 us
  Pallas kernels  70.2 us (95%)
  local copies, waits for them, and re-layouts  2.78 us (4%)
    pallas_call x1, Pallas kernels, shards(): pl.pallas_call(kernel, out_shape=(jax.ShapeDtypeStruct((1, 2, ROWS, D), B...  70.2 us
    unnamed x4, local copies, waits for them, and re-layouts  2.78 us

profile of v1, /device:TPU:1, one launch (start us, length us, event | category | flops | bytes accessed | tf_op | source)
XLA Modules:
  0.0 73.6 jit_solution(452149667909889494)
XLA Ops:
  0.6 70.2 %rollout.1 = (bf16[1,2,256,1024]{3,2,1,0:T(8,128)(2,1)}, f32[1,8]{1,0:T(1,128)}) custom-call(bf16[2,256,1024]{2,1,0:T(8,128)(2,1)} %state.1, f32[1,1024]{1,0:T(1,128)} %bitcast.3, bf16[1024,1024]{1,0:T(8,128)(2,1)} %w_query.1, bf16[1024,1024]{1,0:T(8,128)(2,1)} %w_key.1, bf16[1024,1024]{1,0:T(8,128)(2,1)} %w_value.1, bf16[1024,1024]{1,0:T(8,128)(2,1)} %w_out.1, ...), custom_call_target="tpu_custom_call" | custom-call | tf_op jit(solution)/shard_map/rollout/pallas_call | solution.py:407
  70.9 0.0 copy-start
  70.9 2.3 %copy.16 = bf16[1,2,256,1024]{3,2,1,0:T(8,128)(2,1)} copy(bf16[1,2,256,1024]{3,2,1,0:T(8,128)(2,1)} %get-tuple-element.4) | data formatting | bytes 2097152
  73.1 0.0 copy-done
  73.1 0.5 copy.17
Async XLA Ops:
  70.9 2.3 %copy-start = (f32[1,8]{1,0:T(1,128)S(1)}, f32[1,8]{1,0:T(1,128)}, u32[]{:S(2)}) copy-start(f32[1,8]{1,0:T(1,128)} %get-tuple-element.5) | copy-start | bytes 100

commit v2 on v1

--- a/solution.py
+++ b/solution.py
@@ -17,7 +17,7 @@
 SLOTS = 4
 STEPS = 2
 ALPHA = 0.95
-CHUNKS = 4
+CHUNKS = 8
 CHUNK = ROWS // CHUNKS
 TILE = 256
 SHARE = 32
@@ -67,17 +67,18 @@
     ]
 
     def own_chunk(i):
-        part = pl.ds(i * CHUNK, CHUNK)
+        part = pl.ds(pl.multiple_of(i * CHUNK, CHUNK), CHUNK)
         return pltpu.make_async_copy(state.at[xl, part], cur.at[0, part], xr.at[i])
 
     def x_chunk(i):
-        part = pl.ds(i * CHUNK, CHUNK)
+        part = pl.ds(pl.multiple_of(i * CHUNK, CHUNK), CHUNK)
         return pltpu.make_async_remote_copy(
-            state.at[1 - xl, part], cur.at[0, part], xs.at[i], xr.at[i], device_id=partner, device_id_type=MESH
+            state.at[1 - xl, part], cur.at[0, part], xs.at[i], xr.at[i],
+            device_id={"space": 2 * z + 1 - xl, "step": xl}, device_id_type=MESH,
         )
 
     def z_part(t, i, size):
-        part = pl.ds(i * size, size)
+        part = pl.ds(pl.multiple_of(i * size, size), size)
         return pltpu.make_async_remote_copy(
             cur.at[t, part], halo.at[t, part], zs.at[t, i], zr.at[t, i], device_id=z_target, device_id_type=MESH
         )
@@ -87,22 +88,21 @@
             meta_v.at[0], meta_v.at[1], ms.at[0], mr.at[0], device_id=partner, device_id_type=MESH
         )
 
-    def kv_copy(t, j):
+    def kv_copy(t, j, b):
         return pltpu.make_async_remote_copy(
-            qkvs[t].at[j, pl.ds(2, 2)],
-            qkvs[t].at[j, pl.ds(4 * c, 2)],
-            ks.at[t, j - 1], kr.at[t, j - 1], device_id=other, device_id_type=MESH,
+            qkvs[t].at[j, 2 + b], qkvs[t].at[j, 4 * c + b], ks.at[t, j - 1, b], kr.at[t, j - 1, b],
+            device_id=other, device_id_type=MESH,
         )
 
     def out_remote(t, b, slot):
-        part = pl.ds(b * BLOCK, BLOCK)
+        part = pl.ds(pl.multiple_of(b * BLOCK, BLOCK), BLOCK)
         return pltpu.make_async_remote_copy(
             cur.at[t + 1, part], out.at[0, slot, part], osend.at[t, b], orecv.at[slot, b],
             device_id={"space": 2 * z + c, "step": t}, device_id_type=MESH,
         )
 
     def out_local(t, b, slot):
-        part = pl.ds(b * BLOCK, BLOCK)
+        part = pl.ds(pl.multiple_of(b * BLOCK, BLOCK), BLOCK)
         return pltpu.make_async_copy(cur.at[t + 1, part], out.at[0, slot, part], orecv.at[slot, b])
 
     def preds_copy(t, i):
@@ -161,52 +161,38 @@
 
     pl.semaphore_wait(barrier, 37 + has_z.astype(jnp.int32))
 
+    for i in range(CHUNKS // 2):
+        x_chunk(2 * i + foreign.astype(jnp.int32)).start()
+
     @pl.when(local)
     def _():
-        for i in range(CHUNKS):
-            x_chunk(i).start()
         meta_copy().start()
         to_scalars = pltpu.make_async_copy(meta_v.at[0], meta_s, lsem.at[9])
         to_scalars.start()
         to_scalars.wait()
         used_v[...] = meta_v[0, 2:4, :]
 
-    for i in range(CHUNKS):
+    def forward(i):
         own_chunk(i).wait()
 
         @pl.when(has_z)
         def _():
             z_part(0, i, CHUNK).start()
 
-    @pl.when(foreign)
-    def _():
-        meta_copy().wait_recv()
-        to_scalars = pltpu.make_async_copy(meta_v.at[1], meta_s, lsem.at[9])
-        to_scalars.start()
-        to_scalars.wait()
-        used_v[...] = meta_v[1, 2:4, :]
-
-    loads[5].wait()
-
     def normalise(src, row, rows, dst):
         def step(i, _):
-            part = pl.ds(pl.multiple_of(row + i * 32, 32), 32)
+            part = pl.ds(pl.multiple_of(row + i * 64, 64), 64)
             values = src[part, :].astype(F32)
             factor = lax.rsqrt(jnp.mean(values * values, axis=-1, keepdims=True) + 1e-06)
             dst[part, :] = (values * factor * gains[...]).astype(BF)
             return 0
 
-        lax.fori_loop(0, rows // 32, step, 0)
+        lax.fori_loop(0, rows // 64, step, 0)
 
     def project(row, rows, w, dst, dst_block):
-        def step(n, _):
-            cols = pl.ds(pl.multiple_of(n * TILE, TILE), TILE)
-            values = dot(nrm[pl.ds(row, rows), :], wbuf[w, :, cols]).astype(BF)
-            for i in range(rows // BLOCK):
-                dst[w, dst_block + i, :, cols] = values[i * BLOCK : (i + 1) * BLOCK]
-            return 0
-
-        lax.fori_loop(0, D // TILE, step, 0)
+        values = dot(nrm[pl.ds(row, rows), :], wbuf[w]).astype(BF)
+        for i in range(rows // BLOCK):
+            dst[w, dst_block + i] = values[i * BLOCK : (i + 1) * BLOCK]
 
     first_block = 4 * z + 2 * c - 2
     head_of = lax.broadcasted_iota(jnp.int32, (1, TILE), 1)
@@ -217,21 +203,26 @@
 
     def attend(qkv, b):
         near = [jnp.clip(meta_s[0, b * SLOTS + slot] - first_block, 0, 5) for slot in range(SLOTS)]
-        used = used_v[b : b + 1, :]
+        used = used_v[pl.ds(b, 1), :]
         bias = [jnp.where(used > slot, 0.0, -1e30) for slot in range(SLOTS)]
 
-        def step(g, _):
-            cols = pl.ds(pl.multiple_of(g * TILE, TILE), TILE)
+        def scores(g):
+            cols = slice(g * TILE, (g + 1) * TILE)
             query = qkv[0, 2 + b, :, cols]
             query = jnp.concatenate([query * mask for mask in masks], axis=0)
             keys = [jnp.concatenate([qkv[1, near[i + k], :, cols] for k in range(2)], axis=0) for i in (0, 2)]
-            values = jnp.concatenate([qkv[2, near[i], :, cols] for i in range(SLOTS)], axis=0)
             first = dot_t(query, keys[0])
             second = dot_t(query, keys[1])
             second = jnp.concatenate([second[:, :BLOCK] + bias[2], second[:, BLOCK:] + bias[3]], axis=1)
-            scores = jnp.concatenate([first, second], axis=1)
-            highest = jnp.max(scores, axis=-1, keepdims=True)
-            raised = jnp.exp(scores - highest)
+            return jnp.concatenate([first, second], axis=1)
+
+        ready = scores(0)
+        for g in range(D // TILE):
+            later = scores(g + 1) if g + 1 < D // TILE else None
+            cols = slice(g * TILE, (g + 1) * TILE)
+            values = jnp.concatenate([qkv[2, near[i], :, cols] for i in range(SLOTS)], axis=0)
+            highest = jnp.max(ready, axis=-1, keepdims=True)
+            raised = jnp.exp(ready - highest)
             total = jnp.sum(raised, axis=-1, keepdims=True)
             mixed = dot(raised.astype(BF), values) * (1.0 / total)
             parts = [mixed[i * BLOCK : (i + 1) * BLOCK] for i in range(4)]
@@ -239,31 +230,64 @@
             for i in (2, 1, 0):
                 attended = jnp.where(lane < HEAD * (i + 1), parts[i], attended)
             att[:, cols] = attended.astype(BF)
-            return 0
-
-        lax.fori_loop(0, D // TILE, step, 0)
+            ready = later
 
     def update(t, b):
-        part = pl.ds(b * BLOCK, BLOCK)
-
-        def step(n, _):
-            cols = pl.ds(pl.multiple_of(n * TILE, TILE), TILE)
-            values = cur[t, part, cols].astype(F32) + dot(att[...], wbuf[3, :, cols])
-            cur[t + 1, part, cols] = values.astype(BF)
-            return 0
-
-        lax.fori_loop(0, D // TILE, step, 0)
+        part = pl.ds(pl.multiple_of(b * BLOCK, BLOCK), BLOCK)
+        cur[t + 1, part, :] = (cur[t, part, :].astype(F32) + dot(att[...], wbuf[3])).astype(BF)
+
+    def decode(t):
+        preds[t] = dot(cur[t + 1], wdec[...]).astype(BF)
+        for i in range(8):
+            own = local & (c == t) & (m == i)
+
+            @pl.when(own)
+            def _():
+                preds_own(t, i).start()
+
+            @pl.when(jnp.logical_not(own))
+            def _():
+                preds_copy(t, i).start()
 
     for t in range(STEPS):
         qkv = qkvs[t]
         out_here = local & (c == t)
-        normalise(cur.at[t], 0, ROWS, nrm)
-        for j in (1, 2, 0):
-            if t == 0:
-                loads[(2, 0, 1)[j]].wait()
-            project(0, ROWS, j, qkv, 2)
-            if j:
-                kv_copy(t, j).start()
+        if t == 0:
+            for i in range(4):
+                forward(i)
+            loads[5].wait()
+            normalise(cur.at[0], 0, BLOCK, nrm)
+            forward(4)
+            for j, load, chunk in ((1, 0, 5), (2, 1, 6), (0, 2, 7)):
+                loads[load].wait()
+                project(0, BLOCK, j, qkv, 2)
+                if j:
+                    kv_copy(0, j, 0).start()
+                forward(chunk)
+            normalise(cur.at[0], BLOCK, BLOCK, nrm)
+            for j in (1, 2, 0):
+                project(BLOCK, BLOCK, j, qkv, 3)
+                if j:
+                    kv_copy(0, j, 1).start()
+
+            @pl.when(foreign)
+            def _():
+                meta_copy().wait_recv()
+                to_scalars = pltpu.make_async_copy(meta_v.at[1], meta_s, lsem.at[9])
+                to_scalars.start()
+                to_scalars.wait()
+                used_v[...] = meta_v[1, 2:4, :]
+
+        else:
+            normalise(cur.at[t], 0, ROWS, nrm)
+            for j in (1, 2, 0):
+                project(0, ROWS, j, qkv, 2)
+                if j:
+                    for b in range(2):
+                        kv_copy(t, j, b).start()
+            loads[4].wait()
+            decode(t - 1)
+
         size = CHUNK if t == 0 else BLOCK
         for b in range(2):
 
@@ -276,10 +300,12 @@
             for j in (1, 2):
                 project(b * BLOCK, BLOCK, j, qkv, 4 * c + b)
         for j in (1, 2):
-            kv_copy(t, j).wait_recv()
+            for b in range(2):
+                kv_copy(t, j, b).wait_recv()
         if t == 0:
             loads[3].wait()
-        for b in range(2):
+
+        def block(b, _):
             attend(qkv, b)
             update(t, b)
             if t + 1 < STEPS:
@@ -296,19 +322,10 @@
             def _():
                 out_remote(t, b, xl).start()
 
-        if t == 0:
-            loads[4].wait()
-        preds[t] = dot(cur[t + 1], wdec[...]).astype(BF)
-        for i in range(8):
-            own = out_here & (m == i)
-
-            @pl.when(own)
-            def _():
-                preds_own(t, i).start()
-
-            @pl.when(jnp.logical_not(own))
-            def _():
-                preds_copy(t, i).start()
+            return 0
+
+        lax.fori_loop(0, 2, block, 0)
+    decode(STEPS - 1)
 
     for copy in loads[6:9]:
         copy.wait()
@@ -364,10 +381,11 @@
         for b in range(2):
             out_local(0, b, slot_xl).wait()
 
+    for i in range(CHUNKS // 2):
+        x_chunk(2 * i + foreign.astype(jnp.int32)).wait_send()
+
     @pl.when(local)
     def _():
-        for i in range(CHUNKS):
-            x_chunk(i).wait_send()
         meta_copy().wait_send()
 
     @pl.when(has_z)
@@ -380,7 +398,8 @@
     for t in range(STEPS):
         out_here = local & (c == t)
         for j in (1, 2):
-            kv_copy(t, j).wait_send()
+            for b in range(2):
+                kv_copy(t, j, b).wait_send()
 
         @pl.when(jnp.logical_not(out_here))
         def _():
@@ -407,7 +426,7 @@
     return pl.pallas_call(
         kernel,
         out_shape=(
-            jax.ShapeDtypeStruct((1, 2, ROWS, D), BF),
+            pltpu.VMEM((1, 2, ROWS, D), BF),
             jax.ShapeDtypeStruct((1, GROUPS), F32),
         ),
         in_specs=[anywhere] * 7 + [scalars] * 2 + [anywhere] * 3,
@@ -437,8 +456,8 @@
             dma((CHUNKS,)),
             dma((STEPS, CHUNKS)),
             dma((STEPS, CHUNKS)),
-            dma((STEPS, 2)),
-            dma((STEPS, 2)),
+            dma((STEPS, 2, 2)),
+            dma((STEPS, 2, 2)),
             dma((STEPS, 2)),
             dma((2, 2)),
             dma((STEPS, 8)),

time: 73.8 us -> 55.2 us (0.75)
  Pallas kernels: 70.2 us -> 52.9 us
  local copies, waits for them, and re-layouts: 2.78 us -> 1.49 us
    pallas_call x1, Pallas kernels: 70.2 us -> 52.9 us  [shards(): pl.pallas_call(kernel, out_shape=(pltpu.VMEM((1, 2, ROWS, D), BF), jax.Sh...]
    unnamed x4, local copies, waits for them, and re-layouts: 2.78 us -> 1.49 us
where the time goes in v2:
time: 55.2 us; the launch traced here: 55.1 us
  Pallas kernels  52.9 us (96%)
  local copies, waits for them, and re-layouts  1.49 us (3%)
  between operations  0.65 us (1%)
    pallas_call x1, Pallas kernels, shards(): pl.pallas_call(kernel, out_shape=(pltpu.VMEM((1, 2, ROWS, D), BF), jax.Sh...  52.9 us
    unnamed x4, local copies, waits for them, and re-layouts  1.49 us

profile of v2, /device:TPU:1, one launch (start us, length us, event | category | flops | bytes accessed | tf_op | source)
XLA Modules:
  0.0 55.1 jit_solution(17372845496062158420)
XLA Ops:
  0.6 52.9 %rollout.1 = (bf16[1,2,256,1024]{3,2,1,0:T(8,128)(2,1)S(1)}, f32[1,8]{1,0:T(1,128)}) custom-call(bf16[2,256,1024]{2,1,0:T(8,128)(2,1)} %state.1, f32[1,1024]{1,0:T(1,128)} %bitcast.3, bf16[1024,1024]{1,0:T(8,128)(2,1)} %w_query.1, bf16[1024,1024]{1,0:T(8,128)(2,1)} %w_key.1, bf16[1024,1024]{1,0:T(8,128)(2,1)} %w_value.1, bf16[1024,1024]{1,0:T(8,128)(2,1)} %w_out.1, ...), custom_call_target="tpu_custom_call" | custom-call | tf_op jit(solution)/shard_map/rollout/pallas_call | solution.py:426
  53.6 0.0 copy-start
  53.6 1.0 %copy.16 = bf16[1,2,256,1024]{3,2,1,0:T(8,128)(2,1)} copy(bf16[1,2,256,1024]{3,2,1,0:T(8,128)(2,1)S(1)} %get-tuple-element.2) | data formatting | bytes 2097152
  54.5 0.0 copy-done
  54.5 0.5 copy.17
Async XLA Ops:
  53.6 1.0 %copy-start = (f32[1,8]{1,0:T(1,128)S(1)}, f32[1,8]{1,0:T(1,128)}, u32[]{:S(2)}) copy-start(f32[1,8]{1,0:T(1,128)} %get-tuple-element.7) | copy-start | bytes 100

commit v3 on v2

--- a/solution.py
+++ b/solution.py
@@ -20,7 +20,7 @@
 CHUNKS = 8
 CHUNK = ROWS // CHUNKS
 TILE = 256
-SHARE = 32
+SHARE = 16
 MESH = pl.DeviceIdType.MESH
 BF = jnp.bfloat16
 F32 = jnp.float32
@@ -63,7 +63,8 @@
         fetch(5, gain, gains),
         fetch(6, group_ids, groups),
         fetch(7, area, areas),
-        fetch(8, truth.at[0, pl.ds(pl.multiple_of(m * SHARE, SHARE), SHARE)], goal),
+        fetch(8, truth.at[0, pl.ds(pl.multiple_of(m * SHARE, SHARE), SHARE)], goal.at[0]),
+        fetch(9, truth.at[0, pl.ds(pl.multiple_of(BLOCK + m * SHARE, SHARE), SHARE)], goal.at[1]),
     ]
 
     def own_chunk(i):
@@ -105,14 +106,16 @@
         part = pl.ds(pl.multiple_of(b * BLOCK, BLOCK), BLOCK)
         return pltpu.make_async_copy(cur.at[t + 1, part], out.at[0, slot, part], orecv.at[slot, b])
 
-    def preds_copy(t, i):
+    def preds_copy(t, b, i):
         return pltpu.make_async_remote_copy(
-            preds.at[t, pl.ds(i * SHARE, SHARE)], gathered.at[2 * m + xl], ps.at[t, i], pr.at[0],
+            preds.at[t, b, pl.ds(i * SHARE, SHARE)], gathered.at[b, 2 * m + xl], ps.at[t, b, i], pr.at[0],
             device_id={"member": i, "space": 2 * z + c, "step": t}, device_id_type=MESH,
         )
 
-    def preds_own(t, i):
-        return pltpu.make_async_copy(preds.at[t, pl.ds(i * SHARE, SHARE)], gathered.at[2 * m + xl], pr.at[0])
+    def preds_own(t, b, i):
+        return pltpu.make_async_copy(
+            preds.at[t, b, pl.ds(i * SHARE, SHARE)], gathered.at[b, 2 * m + xl], pr.at[0]
+        )
 
     barrier = pltpu.get_barrier_semaphore()
 
@@ -131,8 +134,7 @@
 
     lax.fori_loop(1, 32, greet_plane, 0)
     for dz in range(1, 4):
-        for x_mate in range(2):
-            greet(space=2 * lax.rem(z + dz, 4) + x_mate)
+        greet(space=2 * lax.rem(z + dz, 4) + xl)
 
     @pl.when(has_z)
     def _():
@@ -159,7 +161,7 @@
     def _():
         halo[...] = jnp.zeros_like(halo)
 
-    pl.semaphore_wait(barrier, 37 + has_z.astype(jnp.int32))
+    pl.semaphore_wait(barrier, 34 + has_z.astype(jnp.int32))
 
     for i in range(CHUNKS // 2):
         x_chunk(2 * i + foreign.astype(jnp.int32)).start()
@@ -167,7 +169,7 @@
     @pl.when(local)
     def _():
         meta_copy().start()
-        to_scalars = pltpu.make_async_copy(meta_v.at[0], meta_s, lsem.at[9])
+        to_scalars = pltpu.make_async_copy(meta_v.at[0], meta_s, lsem.at[10])
         to_scalars.start()
         to_scalars.wait()
         used_v[...] = meta_v[0, 2:4, :]
@@ -236,18 +238,19 @@
         part = pl.ds(pl.multiple_of(b * BLOCK, BLOCK), BLOCK)
         cur[t + 1, part, :] = (cur[t, part, :].astype(F32) + dot(att[...], wbuf[3])).astype(BF)
 
-    def decode(t):
-        preds[t] = dot(cur[t + 1], wdec[...]).astype(BF)
+    def decode(t, b):
+        part = pl.ds(pl.multiple_of(b * BLOCK, BLOCK), BLOCK)
+        preds[t, b] = dot(cur[t + 1, part, :], wdec[...]).astype(BF)
         for i in range(8):
             own = local & (c == t) & (m == i)
 
             @pl.when(own)
             def _():
-                preds_own(t, i).start()
+                preds_own(t, b, i).start()
 
             @pl.when(jnp.logical_not(own))
             def _():
-                preds_copy(t, i).start()
+                preds_copy(t, b, i).start()
 
     for t in range(STEPS):
         qkv = qkvs[t]
@@ -273,7 +276,7 @@
             @pl.when(foreign)
             def _():
                 meta_copy().wait_recv()
-                to_scalars = pltpu.make_async_copy(meta_v.at[1], meta_s, lsem.at[9])
+                to_scalars = pltpu.make_async_copy(meta_v.at[1], meta_s, lsem.at[10])
                 to_scalars.start()
                 to_scalars.wait()
                 used_v[...] = meta_v[1, 2:4, :]
@@ -285,9 +288,6 @@
                 if j:
                     for b in range(2):
                         kv_copy(t, j, b).start()
-            loads[4].wait()
-            decode(t - 1)
-
         size = CHUNK if t == 0 else BLOCK
         for b in range(2):
 
@@ -299,6 +299,10 @@
             normalise(halo.at[t], b * BLOCK, BLOCK, nrm)
             for j in (1, 2):
                 project(b * BLOCK, BLOCK, j, qkv, 4 * c + b)
+            if t == 1 and b == 0:
+                loads[4].wait()
+                for k in range(2):
+                    decode(0, k)
         for j in (1, 2):
             for b in range(2):
                 kv_copy(t, j, b).wait_recv()
@@ -314,6 +318,9 @@
                 def _():
                     z_part(t + 1, b, BLOCK).start()
 
+            if t + 1 == STEPS:
+                decode(t, b)
+
             @pl.when(out_here)
             def _():
                 out_local(t, b, xl).start()
@@ -325,51 +332,55 @@
             return 0
 
         lax.fori_loop(0, 2, block, 0)
-    decode(STEPS - 1)
-
-    for copy in loads[6:9]:
+
+    for copy in loads[6:10]:
         copy.wait()
     pltpu.make_async_copy(gathered, gathered, pr.at[0]).wait()
     epsilon = (1.0 - ALPHA) / MEMBERS
     weighted = jnp.zeros((1, VARS), F32)
-    mine = lax.broadcasted_iota(jnp.int32, (SHARE, ROWS), 0) + m * SHARE
-    spread_out = jnp.where(lax.broadcasted_iota(jnp.int32, (SHARE, ROWS), 1) == mine, areas[...], 0.0)
-    weights = jnp.sum(spread_out, axis=1, keepdims=True)
-    for i in range(SHARE // 16):
-        part = slice(i * 16, i * 16 + 16)
-        values = [gathered[k, part, :].astype(F32) for k in range(MEMBERS)]
-        wanted = goal[part, :].astype(F32)
-        skill = jnp.zeros((16, VARS), F32)
-        spread = jnp.zeros((16, VARS), F32)
+    place = lax.broadcasted_iota(jnp.int32, (SHARE, ROWS), 1) - lax.broadcasted_iota(jnp.int32, (SHARE, ROWS), 0)
+    area_sum = jnp.zeros((1, 1), F32)
+    for b in range(2):
+        weights = jnp.where(place == b * BLOCK + m * SHARE, areas[...], 0.0)
+        weights = jnp.sum(weights, axis=1, keepdims=True)
+        area_sum += jnp.sum(weights, axis=0, keepdims=True)
+        values = [gathered[b, k].astype(F32) for k in range(MEMBERS)]
+        wanted = goal[b].astype(F32)
+        skill = jnp.zeros((SHARE, VARS), F32)
+        spread = jnp.zeros((SHARE, VARS), F32)
         for k in range(MEMBERS):
             skill += jnp.abs(values[k] - wanted)
             for j in range(k):
                 spread += jnp.abs(values[k] - values[j])
         terms = skill * (1.0 / MEMBERS) - spread * ((1.0 - epsilon) / (MEMBERS * (MEMBERS - 1)))
-        weighted += jnp.sum(terms * weights[part], axis=0, keepdims=True)
+        weighted += jnp.sum(terms * weights, axis=0, keepdims=True)
     row = lax.broadcasted_iota(jnp.int32, (8, VARS), 0)
-    tile = jnp.where(row == 0, weighted, jnp.where(row == 1, jnp.sum(weights, axis=0, keepdims=True), 0.0))
-
-    def exchange(tile, buffer, send, recv, me, axis):
+    tile = jnp.where(row == 0, weighted, jnp.where(row == 1, area_sum, 0.0))
+
+    def exchange(tile, buffer, send, recv, me, device):
+        count = buffer.shape[0]
         buffer[me] = tile
 
         def copy(i):
             return pltpu.make_async_remote_copy(
                 buffer.at[me], buffer.at[me], send.at[i - 1], recv.at[0],
-                device_id={axis: lax.rem(me + i, 8)}, device_id_type=MESH,
+                device_id=device(lax.rem(me + i, count)), device_id_type=MESH,
             )
 
-        for i in range(1, 8):
+        for i in range(1, count):
             copy(i).start()
-        rest = buffer.at[pl.ds(0, 7)]
+        rest = buffer.at[pl.ds(0, count - 1)]
         pltpu.make_async_copy(rest, rest, recv.at[0]).wait()
         total = buffer[0]
-        for i in range(1, 8):
+        for i in range(1, count):
             total += buffer[i]
         return total, copy
 
-    tile, copy1 = exchange(tile, red1, r1s, r1r, m, "member")
-    tile, copy2 = exchange(tile, red2, r2s, r2r, s, "space")
+    def in_plane(i):
+        return {"member": lax.div(i, 2), "space": 2 * z + lax.rem(i, 2)}
+
+    tile, copy1 = exchange(tile, red1, r1s, r1r, 2 * m + xl, in_plane)
+    tile, copy2 = exchange(tile, red2, r2s, r2r, z, lambda i: {"space": 2 * i + xl})
     slot = lax.broadcasted_iota(jnp.int32, (1, GROUPS), 1)
     result = jnp.zeros((1, GROUPS), F32)
     for g in range(GROUPS):
@@ -410,10 +421,12 @@
 
             @pl.when(jnp.logical_not(out_here & (m == i)))
             def _():
-                preds_copy(t, i).wait_send()
-
-    for i in range(1, 8):
+                for b in range(2):
+                    preds_copy(t, b, i).wait_send()
+
+    for i in range(1, 16):
         copy1(i).wait_send()
+    for i in range(1, 4):
         copy2(i).wait_send()
 
 
@@ -427,7 +440,7 @@
         kernel,
         out_shape=(
             pltpu.VMEM((1, 2, ROWS, D), BF),
-            jax.ShapeDtypeStruct((1, GROUPS), F32),
+            pltpu.VMEM((1, GROUPS), F32),
         ),
         in_specs=[anywhere] * 7 + [scalars] * 2 + [anywhere] * 3,
         out_specs=(anywhere, pl.BlockSpec(memory_space=pltpu.VMEM)),
@@ -440,18 +453,18 @@
             pltpu.VMEM((3, 6, BLOCK, D), BF),
             pltpu.VMEM((3, 6, BLOCK, D), BF),
             pltpu.VMEM((BLOCK, D), BF),
-            pltpu.VMEM((STEPS, ROWS, VARS), BF),
-            pltpu.VMEM((MEMBERS, SHARE, VARS), BF),
-            pltpu.VMEM((SHARE, VARS), BF),
+            pltpu.VMEM((STEPS, 2, BLOCK, VARS), BF),
+            pltpu.VMEM((2, MEMBERS, SHARE, VARS), BF),
+            pltpu.VMEM((2, SHARE, VARS), BF),
             pltpu.VMEM((1, D), F32),
             pltpu.VMEM((1, VARS), jnp.int32),
             pltpu.VMEM((1, ROWS), F32),
             pltpu.VMEM((2, 8, 128), jnp.int32),
             pltpu.VMEM((2, 128), jnp.int32),
             pltpu.SMEM((8, 128), jnp.int32),
-            pltpu.VMEM((8, 8, VARS), F32),
-            pltpu.VMEM((8, 8, VARS), F32),
-            dma((10,)),
+            pltpu.VMEM((16, 8, VARS), F32),
+            pltpu.VMEM((4, 8, VARS), F32),
+            dma((11,)),
             dma((CHUNKS,)),
             dma((CHUNKS,)),
             dma((STEPS, CHUNKS)),
@@ -460,13 +473,13 @@
             dma((STEPS, 2, 2)),
             dma((STEPS, 2)),
             dma((2, 2)),
-            dma((STEPS, 8)),
+            dma((STEPS, 2, 8)),
             dma((1,)),
             dma((1,)),
             dma((1,)),
-            dma((7,)),
+            dma((15,)),
             dma((1,)),
-            dma((7,)),
+            dma((3,)),
             dma((1,)),
         ],
         compiler_params=pltpu.CompilerParams(

time: 55.2 us -> 52.9 us (0.958)
  Pallas kernels: 52.9 us -> 50.7 us
    pallas_call x1, Pallas kernels: 52.9 us -> 50.7 us  [shards(): pl.pallas_call(kernel, out_shape=(pltpu.VMEM((1, 2, ROWS, D), BF), pltpu....]
    unnamed x4 -> x2, local copies, waits for them, and re-layouts: 1.49 us -> 1.48 us
where the time goes in v3:
time: 52.9 us; the launch traced here: 52.8 us
  Pallas kernels  50.7 us (96%)
  local copies, waits for them, and re-layouts  1.48 us (3%)
  between operations  0.64 us (1%)
    pallas_call x1, Pallas kernels, shards(): pl.pallas_call(kernel, out_shape=(pltpu.VMEM((1, 2, ROWS, D), BF), pltpu....  50.7 us
    unnamed x2, local copies, waits for them, and re-layouts  1.48 us

profile of v3, /device:TPU:1, one launch (start us, length us, event | category | flops | bytes accessed | tf_op | source)
XLA Modules:
  0.0 52.8 jit_solution(10760116786029463651)
XLA Ops:
  0.6 50.7 %rollout.1 = (bf16[1,2,256,1024]{3,2,1,0:T(8,128)(2,1)S(1)}, f32[1,8]{1,0:T(1,128)S(1)}) custom-call(bf16[2,256,1024]{2,1,0:T(8,128)(2,1)} %state.1, f32[1,1024]{1,0:T(1,128)} %bitcast.3, bf16[1024,1024]{1,0:T(8,128)(2,1)} %w_query.1, bf16[1024,1024]{1,0:T(8,128)(2,1)} %w_key.1, bf16[1024,1024]{1,0:T(8,128)(2,1)} %w_value.1, bf16[1024,1024]{1,0:T(8,128)(2,1)} %w_out.1, ...), custom_call_target="tpu_custom_call" | custom-call | tf_op jit(solution)/shard_map/rollout/pallas_call | solution.py:439
  51.3 1.0 %copy.16 = bf16[1,2,256,1024]{3,2,1,0:T(8,128)(2,1)} copy(bf16[1,2,256,1024]{3,2,1,0:T(8,128)(2,1)S(1)} %get-tuple-element.2) | data formatting | bytes 2097152
  52.3 0.5 copy.17

commit v4 on v3

--- a/solution.py
+++ b/solution.py
@@ -21,6 +21,7 @@
 CHUNK = ROWS // CHUNKS
 TILE = 256
 SHARE = 16
+ROUNDS = 5
 MESH = pl.DeviceIdType.MESH
 BF = jnp.bfloat16
 F32 = jnp.float32
@@ -38,8 +39,8 @@
     state, gain, w_query, w_key, w_value, w_out, w_decode, neighbours, counts, group_ids, area, truth,
     out, loss,
     cur, halo, nrm, wbuf, wdec, qkv0, qkv1, att, preds, gathered, goal, gains, groups, areas, meta_v, used_v, meta_s,
-    red1, red2,
-    lsem, xs, xr, zs, zr, ks, kr, osend, orecv, ps, pr, ms, mr, r1s, r1r, r2s, r2r,
+    red,
+    lsem, xs, xr, zs, zr, ks, kr, osend, orecv, ps, pr, ms, mr, rs, rr, rounds,
 ):
     m, s, c = (lax.axis_index(name) for name in ("member", "space", "step"))
     z, xl = lax.div(s, 2), lax.rem(s, 2)
@@ -119,34 +120,55 @@
 
     barrier = pltpu.get_barrier_semaphore()
 
-    def greet(**device):
-        pl.semaphore_signal(barrier, inc=1, device_id=device, device_id_type=MESH)
-
-    for copy in loads[:1]:
-        copy.start()
-
-    def greet_plane(i, _):
-        mate = lax.rem(m + lax.div(i, 4), 8)
-        x_mate = lax.rem(xl + lax.rem(lax.div(i, 2), 2), 2)
-        core = lax.rem(c + lax.rem(i, 2), 2)
-        greet(member=mate, space=2 * z + x_mate, step=core)
-        return 0
-
-    lax.fori_loop(1, 32, greet_plane, 0)
-    for dz in range(1, 4):
-        greet(space=2 * lax.rem(z + dz, 4) + xl)
-
-    @pl.when(has_z)
-    def _():
-        greet(**z_target)
+    x = 2 * lax.rem(m, 2) + xl
+    y = lax.div(m, 2)
+    xs4, ys4, zs4 = ([lax.rem(at + i, 4) for i in range(4)] for at in (x, y, z))
+
+    def chip(dx, dy, dz):
+        return {"member": 2 * ys4[dy] + lax.div(xs4[dx], 2), "space": 2 * zs4[dz] + lax.rem(xs4[dx], 2)}
+
+    x_mate = 2 * z + 1 - xl
+    across = {"member": 2 * y + 1 - lax.rem(m, 2), "space": x_mate}
+    beside = [
+        {"space": x_mate},
+        {"space": x_mate, "step": 1 - c},
+        other,
+        across,
+        chip(0, 1, 0),
+        chip(0, 3, 0),
+        chip(0, 0, 1),
+        chip(0, 0, 3),
+    ]
+    near_count = len(beside) + has_z.astype(jnp.int32)
+
+    def greet(semaphore):
+        for device in beside:
+            pl.semaphore_signal(semaphore, inc=1, device_id=device, device_id_type=MESH)
+
+        @pl.when(has_z)
+        def _():
+            pl.semaphore_signal(semaphore, inc=1, device_id=z_target, device_id_type=MESH)
+
+    def meet(k):
+        if k > 0:
+            pl.semaphore_wait(rounds.at[k - 1], near_count)
+        if k < ROUNDS:
+            greet(rounds.at[k])
+
+    greet(barrier)
 
     @pl.when(local)
     def _():
         for i in range(CHUNKS):
             own_chunk(i).start()
 
-    for copy in loads[1:]:
+    for copy in loads:
         copy.start()
+
+    pl.semaphore_wait(barrier, near_count)
+
+    for i in range(CHUNKS // 2):
+        x_chunk(2 * i + foreign.astype(jnp.int32)).start()
 
     column = lax.broadcasted_iota(jnp.int32, (8, 128), 1)
     row8 = lax.broadcasted_iota(jnp.int32, (8, 128), 0)
@@ -160,11 +182,6 @@
     @pl.when(jnp.logical_not(has_z))
     def _():
         halo[...] = jnp.zeros_like(halo)
-
-    pl.semaphore_wait(barrier, 34 + has_z.astype(jnp.int32))
-
-    for i in range(CHUNKS // 2):
-        x_chunk(2 * i + foreign.astype(jnp.int32)).start()
 
     @pl.when(local)
     def _():
@@ -267,6 +284,7 @@
                 if j:
                     kv_copy(0, j, 0).start()
                 forward(chunk)
+            meet(0)
             normalise(cur.at[0], BLOCK, BLOCK, nrm)
             for j in (1, 2, 0):
                 project(BLOCK, BLOCK, j, qkv, 3)
@@ -282,6 +300,7 @@
                 used_v[...] = meta_v[1, 2:4, :]
 
         else:
+            meet(2)
             normalise(cur.at[t], 0, ROWS, nrm)
             for j in (1, 2, 0):
                 project(0, ROWS, j, qkv, 2)
@@ -300,12 +319,14 @@
             for j in (1, 2):
                 project(b * BLOCK, BLOCK, j, qkv, 4 * c + b)
             if t == 1 and b == 0:
+                meet(3)
                 loads[4].wait()
                 for k in range(2):
                     decode(0, k)
         for j in (1, 2):
             for b in range(2):
                 kv_copy(t, j, b).wait_recv()
+        meet(1 if t == 0 else 4)
         if t == 0:
             loads[3].wait()
 
@@ -354,39 +375,24 @@
                 spread += jnp.abs(values[k] - values[j])
         terms = skill * (1.0 / MEMBERS) - spread * ((1.0 - epsilon) / (MEMBERS * (MEMBERS - 1)))
         weighted += jnp.sum(terms * weights, axis=0, keepdims=True)
-    row = lax.broadcasted_iota(jnp.int32, (8, VARS), 0)
-    tile = jnp.where(row == 0, weighted, jnp.where(row == 1, area_sum, 0.0))
-
-    def exchange(tile, buffer, send, recv, me, device):
-        count = buffer.shape[0]
-        buffer[me] = tile
-
-        def copy(i):
-            return pltpu.make_async_remote_copy(
-                buffer.at[me], buffer.at[me], send.at[i - 1], recv.at[0],
-                device_id=device(lax.rem(me + i, count)), device_id_type=MESH,
-            )
-
-        for i in range(1, count):
-            copy(i).start()
-        rest = buffer.at[pl.ds(0, count - 1)]
-        pltpu.make_async_copy(rest, rest, recv.at[0]).wait()
-        total = buffer[0]
-        for i in range(1, count):
-            total += buffer[i]
-        return total, copy
-
-    def in_plane(i):
-        return {"member": lax.div(i, 2), "space": 2 * z + lax.rem(i, 2)}
-
-    tile, copy1 = exchange(tile, red1, r1s, r1r, 2 * m + xl, in_plane)
-    tile, copy2 = exchange(tile, red2, r2s, r2r, z, lambda i: {"space": 2 * i + xl})
-    slot = lax.broadcasted_iota(jnp.int32, (1, GROUPS), 1)
-    result = jnp.zeros((1, GROUPS), F32)
+    slot = lax.broadcasted_iota(jnp.int32, (1, VARS), 1)
+    line = jnp.where(slot == GROUPS, area_sum, 0.0)
     for g in range(GROUPS):
-        share = jnp.sum(jnp.where(groups[...] == g, tile[0:1], 0.0), axis=1, keepdims=True)
-        result = jnp.where(slot == g, share, result)
-    loss[...] = result / (tile[1:2, :GROUPS] * (VARS // GROUPS))
+        share = jnp.sum(jnp.where(groups[...] == g, weighted, 0.0), axis=1, keepdims=True)
+        line = jnp.where(slot == g, share, line)
+    meet(ROUNDS)
+    place = 8 * m + s
+    red[place] = line
+    steps = [(dx, dy, dz) for dx in range(4) for dy in range(4) for dz in range(4)]
+    steps.sort(key=lambda step: -sum(min(d, 4 - d) for d in step))
+    for step in steps[:-1]:
+        pltpu.make_async_remote_copy(
+            red.at[place], red.at[place], rs.at[0], rr.at[0], device_id=chip(*step), device_id_type=MESH
+        ).start()
+    rest = red.at[pl.ds(0, 63)]
+    pltpu.make_async_copy(rest, rest, rr.at[0]).wait()
+    line = jnp.sum(red[...], axis=0)
+    loss[...] = line[:, :GROUPS] / (line[:, GROUPS : GROUPS + 1] * (VARS // GROUPS))
 
     for slot_xl in range(2):
         for b in range(2):
@@ -424,10 +430,7 @@
                 for b in range(2):
                     preds_copy(t, b, i).wait_send()
 
-    for i in range(1, 16):
-        copy1(i).wait_send()
-    for i in range(1, 4):
-        copy2(i).wait_send()
+    pltpu.make_async_copy(rest, rest, rs.at[0]).wait()
 
 
 def shards(
@@ -462,8 +465,7 @@
             pltpu.VMEM((2, 8, 128), jnp.int32),
             pltpu.VMEM((2, 128), jnp.int32),
             pltpu.SMEM((8, 128), jnp.int32),
-            pltpu.VMEM((16, 8, VARS), F32),
-            pltpu.VMEM((4, 8, VARS), F32),
+            pltpu.VMEM((64, 1, VARS), F32),
             dma((11,)),
             dma((CHUNKS,)),
             dma((CHUNKS,)),
@@ -477,10 +479,9 @@
             dma((1,)),
             dma((1,)),
             dma((1,)),
-            dma((15,)),
             dma((1,)),
-            dma((3,)),
             dma((1,)),
+            pltpu.SemaphoreType.REGULAR((ROUNDS,)),
         ],
         compiler_params=pltpu.CompilerParams(
             collective_id=0, has_side_effects=True, vmem_limit_bytes=60 * 1024 * 1024

time: 52.9 us -> 49.9 us (0.943)
  Pallas kernels: 50.7 us -> 47.7 us
    pallas_call x1, Pallas kernels: 50.7 us -> 47.7 us  [shards(): pl.pallas_call(kernel, out_shape=(pltpu.VMEM((1, 2, ROWS, D), BF), pltpu....]
where the time goes in v4:
time: 49.9 us; the launch traced here: 49.8 us
  Pallas kernels  47.7 us (96%)
  local copies, waits for them, and re-layouts  1.48 us (3%)
  between operations  0.64 us (1%)
    pallas_call x1, Pallas kernels, shards(): pl.pallas_call(kernel, out_shape=(pltpu.VMEM((1, 2, ROWS, D), BF), pltpu....  47.7 us
    unnamed x2, local copies, waits for them, and re-layouts  1.48 us

profile of v4, /device:TPU:1, one launch (start us, length us, event | category | flops | bytes accessed | tf_op | source)
XLA Modules:
  0.0 49.8 jit_solution(4133960981804752631)
XLA Ops:
  0.6 47.7 %rollout.1 = (bf16[1,2,256,1024]{3,2,1,0:T(8,128)(2,1)S(1)}, f32[1,8]{1,0:T(1,128)S(1)}) custom-call(bf16[2,256,1024]{2,1,0:T(8,128)(2,1)} %state.1, f32[1,1024]{1,0:T(1,128)} %bitcast.3, bf16[1024,1024]{1,0:T(8,128)(2,1)} %w_query.1, bf16[1024,1024]{1,0:T(8,128)(2,1)} %w_key.1, bf16[1024,1024]{1,0:T(8,128)(2,1)} %w_value.1, bf16[1024,1024]{1,0:T(8,128)(2,1)} %w_out.1, ...), custom_call_target="tpu_custom_call" | custom-call | tf_op jit(solution)/shard_map/rollout/pallas_call | solution.py:442
  48.3 1.0 %copy.16 = bf16[1,2,256,1024]{3,2,1,0:T(8,128)(2,1)} copy(bf16[1,2,256,1024]{3,2,1,0:T(8,128)(2,1)S(1)} %get-tuple-element.2) | data formatting | bytes 2097152
  49.3 0.5 %copy.17 = f32[1,8]{1,0:T(1,128)} copy(f32[1,8]{1,0:T(1,128)S(1)} %get-tuple-element.3) | data formatting | bytes 64

commit v5 on v4

--- a/solution.py
+++ b/solution.py
@@ -107,16 +107,20 @@
         part = pl.ds(pl.multiple_of(b * BLOCK, BLOCK), BLOCK)
         return pltpu.make_async_copy(cur.at[t + 1, part], out.at[0, slot, part], orecv.at[slot, b])
 
-    def preds_copy(t, b, i):
+    def preds_part(t, b, k):
+        i = lax.rem(m + k, 8)
+        return preds.at[t, b, pl.ds(pl.multiple_of(i * SHARE, SHARE), SHARE)], gathered.at[b, 2 * m + xl], i
+
+    def preds_copy(t, b, k):
+        src, dst, i = preds_part(t, b, k)
         return pltpu.make_async_remote_copy(
-            preds.at[t, b, pl.ds(i * SHARE, SHARE)], gathered.at[b, 2 * m + xl], ps.at[t, b, i], pr.at[0],
+            src, dst, ps.at[t, b, k], pr.at[b],
             device_id={"member": i, "space": 2 * z + c, "step": t}, device_id_type=MESH,
         )
 
-    def preds_own(t, b, i):
-        return pltpu.make_async_copy(
-            preds.at[t, b, pl.ds(i * SHARE, SHARE)], gathered.at[b, 2 * m + xl], pr.at[0]
-        )
+    def preds_own(t, b):
+        src, dst, _ = preds_part(t, b, 0)
+        return pltpu.make_async_copy(src, dst, pr.at[b])
 
     barrier = pltpu.get_barrier_semaphore()
 
@@ -157,6 +161,11 @@
 
     greet(barrier)
 
+    pl.semaphore_wait(barrier, near_count)
+
+    for i in range(CHUNKS // 2):
+        x_chunk(2 * i + foreign.astype(jnp.int32)).start()
+
     @pl.when(local)
     def _():
         for i in range(CHUNKS):
@@ -164,11 +173,6 @@
 
     for copy in loads:
         copy.start()
-
-    pl.semaphore_wait(barrier, near_count)
-
-    for i in range(CHUNKS // 2):
-        x_chunk(2 * i + foreign.astype(jnp.int32)).start()
 
     column = lax.broadcasted_iota(jnp.int32, (8, 128), 1)
     row8 = lax.broadcasted_iota(jnp.int32, (8, 128), 0)
@@ -258,16 +262,17 @@
     def decode(t, b):
         part = pl.ds(pl.multiple_of(b * BLOCK, BLOCK), BLOCK)
         preds[t, b] = dot(cur[t + 1, part, :], wdec[...]).astype(BF)
-        for i in range(8):
-            own = local & (c == t) & (m == i)
-
-            @pl.when(own)
-            def _():
-                preds_own(t, b, i).start()
-
-            @pl.when(jnp.logical_not(own))
-            def _():
-                preds_copy(t, b, i).start()
+        for k in (4, 5, 3, 2, 6, 1, 7):
+            preds_copy(t, b, k).start()
+        own = local & (c == t)
+
+        @pl.when(own)
+        def _():
+            preds_own(t, b).start()
+
+        @pl.when(jnp.logical_not(own))
+        def _():
+            preds_copy(t, b, 0).start()
 
     for t in range(STEPS):
         qkv = qkvs[t]
@@ -356,7 +361,6 @@
 
     for copy in loads[6:10]:
         copy.wait()
-    pltpu.make_async_copy(gathered, gathered, pr.at[0]).wait()
     epsilon = (1.0 - ALPHA) / MEMBERS
     weighted = jnp.zeros((1, VARS), F32)
     place = lax.broadcasted_iota(jnp.int32, (SHARE, ROWS), 1) - lax.broadcasted_iota(jnp.int32, (SHARE, ROWS), 0)
@@ -365,6 +369,7 @@
         weights = jnp.where(place == b * BLOCK + m * SHARE, areas[...], 0.0)
         weights = jnp.sum(weights, axis=1, keepdims=True)
         area_sum += jnp.sum(weights, axis=0, keepdims=True)
+        pltpu.make_async_copy(gathered.at[b], gathered.at[b], pr.at[b]).wait()
         values = [gathered[b, k].astype(F32) for k in range(MEMBERS)]
         wanted = goal[b].astype(F32)
         skill = jnp.zeros((SHARE, VARS), F32)
@@ -423,12 +428,13 @@
             for b in range(2):
                 out_remote(t, b, xl).wait_send()
 
-        for i in range(8):
-
-            @pl.when(jnp.logical_not(out_here & (m == i)))
+        for b in range(2):
+            for k in range(1, 8):
+                preds_copy(t, b, k).wait_send()
+
+            @pl.when(jnp.logical_not(out_here))
             def _():
-                for b in range(2):
-                    preds_copy(t, b, i).wait_send()
+                preds_copy(t, b, 0).wait_send()
 
     pltpu.make_async_copy(rest, rest, rs.at[0]).wait()
 
@@ -476,7 +482,7 @@
             dma((STEPS, 2)),
             dma((2, 2)),
             dma((STEPS, 2, 8)),
-            dma((1,)),
+            dma((2,)),
             dma((1,)),
             dma((1,)),
             dma((1,)),

time: 49.9 us -> 49.7 us (level)
  no operation moved by 1% of the time
where the time goes in v5:
time: 49.7 us; the launch traced here: 49.6 us
  Pallas kernels  47.5 us (96%)
  local copies, waits for them, and re-layouts  1.48 us (3%)
  between operations  0.64 us (1%)
    pallas_call x1, Pallas kernels, shards(): pl.pallas_call(kernel, out_shape=(pltpu.VMEM((1, 2, ROWS, D), BF), pltpu....  47.5 us
    unnamed x2, local copies, waits for them, and re-layouts  1.48 us

profile of v5, /device:TPU:1, one launch (start us, length us, event | category | flops | bytes accessed | tf_op | source)
XLA Modules:
  0.0 49.6 jit_solution(2325059051013758857)
XLA Ops:
  0.6 47.5 %rollout.1 = (bf16[1,2,256,1024]{3,2,1,0:T(8,128)(2,1)S(1)}, f32[1,8]{1,0:T(1,128)S(1)}) custom-call(bf16[2,256,1024]{2,1,0:T(8,128)(2,1)} %state.1, f32[1,1024]{1,0:T(1,128)} %bitcast.3, bf16[1024,1024]{1,0:T(8,128)(2,1)} %w_query.1, bf16[1024,1024]{1,0:T(8,128)(2,1)} %w_key.1, bf16[1024,1024]{1,0:T(8,128)(2,1)} %w_value.1, bf16[1024,1024]{1,0:T(8,128)(2,1)} %w_out.1, ...), custom_call_target="tpu_custom_call" | custom-call | tf_op jit(solution)/shard_map/rollout/pallas_call | solution.py:448
  48.1 1.0 %copy.16 = bf16[1,2,256,1024]{3,2,1,0:T(8,128)(2,1)} copy(bf16[1,2,256,1024]{3,2,1,0:T(8,128)(2,1)S(1)} %get-tuple-element.2) | data formatting | bytes 2097152
  49.1 0.5 %copy.17 = f32[1,8]{1,0:T(1,128)} copy(f32[1,8]{1,0:T(1,128)S(1)} %get-tuple-element.3) | data formatting | bytes 64
